TPU v7x, 32 devices: a whole 2x2x4 slice. The times are simulated.
32 devices in a mesh: groups: 2 (over y), seq: 4 (over z), mp: 4 (over x, core).
Axes of the slice: x: 2, y: 2, z: 4, core: 2. Of those that a mesh axis runs over, the one named last changes fastest.
Arguments:
- tile_features: bfloat16 [1536, 1536], P(('groups', 'seq'), 'mp'), parts along dimension 0, may hold values from -6 to 6
- head_outputs: bfloat16 [1536, 1536], P(('groups', 'seq'), 'mp'), parts along dimension 0, may hold values from -6 to 6
- out_proj: bfloat16 [1536, 1536], P('mp'), may hold values from -0.15625 to 0.15625
- layer_scale: float32 [1536], replicated, may hold values from 0.3 to 1.5
- tile_gain: float32 [1536], replicated, may hold values from 0.5 to 2
- slide_proj: bfloat16 [1536, 768], replicated, may hold values from -0.15625 to 0.15625
- slide_gain: float32 [768], replicated, may hold values from 0.5 to 2
- qkv_weight: bfloat16 [768, 3, 768], P(None, None, 'mp'), may hold values from -1 to 1
- slide_slot: int32 [1536], P('groups'), parts along dimension 0, may hold values from 0 to 767, as said below
- slide_len: int32 [8], P('groups'), parts along dimension 0, may hold values from 1 to 384, 768 in all
- seg_log: int32 [12], replicated, may hold values from 0 to 2, as said below
- rate_log: int32 [12], replicated, may hold values from 0 to 2, as said below
- out_grad: bfloat16 [1536, 768], P(('groups', 'seq'), 'mp'), parts along dimension 0, may hold values from -6 to 6
Outputs:
- slide_heads: bfloat16 [1536, 768], P(('groups', 'seq'), 'mp'), parts along dimension 0
- tile_grad: bfloat16 [1536, 1536], P(('groups', 'seq', 'mp')), parts along dimension 0
- head_grad: bfloat16 [1536, 1536], P(('groups', 'seq'), 'mp'), parts along dimension 0
There are 2 independent parts, one for each index of `groups`. A program takes and returns all parts, laid end to end along the dimension named above; an argument that names none is the same for every part. Nothing has to cross between parts.
Inputs may be any that keep to these rules, and one draw needn't show every extreme that they name: slide_slot is a permutation of the 768 positions. Of the 192 tiles of one index of seq, at most 96 fill positions of any one index of seq (the positions p with the same p // 192); in every draw some index sends exactly 96 to some index. `slide_len`: the slides sum to 768 positions; the longest has exactly 384. `seg_log`: some head has 0 and some head has 2. `rate_log`: some head has 0 and some head has 2.
All inputs are finite; a program needn't handle non-finite values.
Results may differ from a plain program's by a relative error of at most 0.028.
Values may be sent and summed in bfloat16 or wider, within the bound.
A program may use at most 64 MiB of HBM per device.

v0:
```python
import jax
import jax.numpy as jnp
from jax import lax
from jax.sharding import PartitionSpec as P

HEAD_DIM = 64
SPAN_LOG = 2


EPSILON = 1e-06


def swapped(block, axis, distance):
    count = lax.axis_size(axis)
    route = []
    for low in range(count):
        high = low | 1 << distance
        if high != low and high < count:
            route += [(low, high), (high, low)]
    return lax.ppermute(block, axis, route)


def norm_parts(values):
    center = values - jnp.mean(values, axis=-1, keepdims=True)
    inverse = 1.0 / jnp.sqrt(jnp.mean(center * center, axis=-1, keepdims=True) + EPSILON)
    return (center * inverse, inverse)


def norm_back(upstream, normed, inverse):
    first_mean = jnp.mean(upstream, axis=-1, keepdims=True)
    second_mean = jnp.mean(upstream * normed, axis=-1, keepdims=True)
    return inverse * (upstream - first_mean - normed * second_mean)


def slide_ids(positions, slide_len):
    bounds = jnp.cumsum(slide_len)
    return jnp.sum((positions[:, None] >= bounds[None, :]).astype(jnp.int32), axis=1)


def visible(query_pos, key_pos, query_slide, key_slide, widths, strides):
    same_slide = (query_slide[:, None] == key_slide[None, :])[None, :, :]
    window = widths[:, None, None]
    same_window = query_pos[None, :, None] // window == key_pos[None, None, :] // window
    stride = strides[:, None, None]
    same_phase = query_pos[None, :, None] % stride == key_pos[None, None, :] % stride
    return same_slide & same_window & same_phase


def softmax_rows(scores, allowed):
    shifted = jnp.where(allowed, scores, -jnp.inf)
    row_max = jnp.max(shifted, axis=-1, keepdims=True)
    raised = jnp.exp(shifted - row_max)
    return raised / jnp.sum(raised, axis=-1, keepdims=True)


def share_sum(values):
    return lax.psum(values, "mp")


def reroute(buffer):
    return lax.all_to_all(buffer, "seq", split_axis=0, concat_axis=0, tiled=True)


def join_halves(own_part, partner_part, upper_half):
    return jnp.where(
        upper_half,
        jnp.concatenate([partner_part, own_part], axis=1),
        jnp.concatenate([own_part, partner_part], axis=1),
    )


def group_collect(stacked, seq_place):
    for bit_place in range(SPAN_LOG):
        partner_part = swapped(stacked, "seq", bit_place)
        stacked = join_halves(stacked, partner_part, seq_place >> bit_place & 1 == 1)
    return stacked


def group_reduce(stacked, seq_place):
    for bit_place in reversed(range(SPAN_LOG)):
        half_rows = stacked.shape[1] // 2
        upper_half = seq_place >> bit_place & 1 == 1
        lower_part = stacked[:, :half_rows]
        higher_part = stacked[:, half_rows:]
        kept_part = jnp.where(upper_half, higher_part, lower_part)
        given_part = jnp.where(upper_half, lower_part, higher_part)
        stacked = kept_part + swapped(given_part.astype(jnp.bfloat16), "seq", bit_place).astype(
            given_part.dtype
        )
    return stacked


def tile_forward(summed, tile_gain, slide_proj, slide_gain):
    tile_normed, tile_inverse = norm_parts(summed)
    lifted = (tile_normed * tile_gain).astype(jnp.bfloat16)
    embedded = jnp.dot(lifted, slide_proj, preferred_element_type=jnp.float32)
    slide_normed, slide_inverse = norm_parts(embedded)
    entering = (slide_normed * slide_gain).astype(jnp.bfloat16)
    return (entering, (tile_normed, tile_inverse, slide_normed, slide_inverse))


def tile_backward(entering_grad, saved_state, tile_gain, slide_proj, slide_gain, layer_scale):
    tile_normed, tile_inverse, slide_normed, slide_inverse = saved_state
    embedded_grad = norm_back(entering_grad * slide_gain, slide_normed, slide_inverse).astype(
        jnp.bfloat16
    )
    lifted_grad = lax.dot_general(
        embedded_grad, slide_proj, (((1,), (1,)), ((), ())), preferred_element_type=jnp.float32
    )
    summed_grad = norm_back(lifted_grad * tile_gain, tile_normed, tile_inverse)
    mixed_grad = (layer_scale * summed_grad).astype(jnp.bfloat16)
    return (summed_grad, mixed_grad)


def shards(
    tile_features,
    head_outputs,
    out_proj,
    layer_scale,
    tile_gain,
    slide_proj,
    slide_gain,
    qkv_weight,
    slide_slot,
    slide_len,
    seg_log,
    rate_log,
    out_grad,
):
    seq_count = lax.axis_size("seq")
    seq_place = lax.axis_index("seq")
    mp_count = lax.axis_size("mp")
    mp_place = lax.axis_index("mp")
    row_count, width_part = tile_features.shape
    share_rows = row_count // mp_count
    head_cols = qkv_weight.shape[2]
    local_heads = head_cols // HEAD_DIM
    group_size = 1 << SPAN_LOG
    group_count = group_size * row_count
    capacity = 2 * (row_count // seq_count)
    slot_total = seq_count * capacity
    column = mp_place * width_part
    weight_flat = qkv_weight.reshape(qkv_weight.shape[0], 3 * head_cols)
    scale = HEAD_DIM ** (-0.5)
    term = layer_scale * jnp.dot(head_outputs, out_proj, preferred_element_type=jnp.float32)
    own_block = lax.dynamic_slice_in_dim(term, column, width_part, 1) + tile_features.astype(
        jnp.float32
    )
    summed = share_sum(lax.dynamic_update_slice_in_dim(term, own_block, column, 1))
    entering, saved_state = tile_forward(summed, tile_gain, slide_proj, slide_gain)
    projected = jnp.dot(entering, weight_flat, preferred_element_type=jnp.float32).astype(
        jnp.bfloat16
    )
    tile_index = jnp.arange(row_count, dtype=jnp.int32)
    my_slots = lax.dynamic_slice_in_dim(slide_slot, seq_place * row_count, row_count, 0)
    target = my_slots // row_count
    send_rank = jnp.sum(
        ((target[:, None] == target[None, :]) & (tile_index[None, :] < tile_index[:, None])).astype(
            jnp.int32
        ),
        axis=1,
    )
    send_slot = target * capacity + send_rank
    every_tile = jnp.arange(slide_slot.shape[0], dtype=jnp.int32)
    anchor_all = jnp.zeros_like(slide_slot).at[slide_slot].set(every_tile)
    anchor = lax.dynamic_slice_in_dim(anchor_all, seq_place * row_count, row_count, 0)
    anchor_device = anchor // row_count
    anchor_row = anchor % row_count
    recv_rank = jnp.sum(
        (
            (anchor_device[:, None] == anchor_device[None, :])
            & (anchor_row[None, :] < anchor_row[:, None])
        ).astype(jnp.int32),
        axis=1,
    )
    recv_slot = anchor_device * capacity + recv_rank

    def pack(values, slot_list):
        slot_table = jnp.full((slot_total,), row_count, jnp.int32).at[slot_list].set(tile_index)
        padded = jnp.concatenate([values, jnp.zeros((1, values.shape[1]), values.dtype)], axis=0)
        return padded[slot_table].reshape(seq_count, capacity, values.shape[1])

    def unpack(buffer, slot_list):
        return buffer.reshape(slot_total, buffer.shape[2])[slot_list]

    arriving = unpack(reroute(pack(projected, send_slot)), recv_slot)
    queries = arriving[:, :head_cols]
    stacked = group_collect(
        jnp.stack([arriving[:, head_cols : 2 * head_cols], arriving[:, 2 * head_cols :]]), seq_place
    )
    keys_all = stacked[0].reshape(group_count, local_heads, HEAD_DIM)
    values_all = stacked[1].reshape(group_count, local_heads, HEAD_DIM)
    query_heads = queries.reshape(row_count, local_heads, HEAD_DIM)
    here_pos = seq_place * row_count + tile_index
    group_first = seq_place // group_size * group_count
    group_pos = group_first + jnp.arange(group_count, dtype=jnp.int32)
    here_slide = slide_ids(here_pos, slide_len)
    group_slide = slide_ids(group_pos, slide_len)
    head_start = mp_place * local_heads
    widths = row_count * jnp.left_shift(
        jnp.int32(1), lax.dynamic_slice_in_dim(seg_log, head_start, local_heads, 0)
    )
    strides = jnp.left_shift(
        jnp.int32(1), lax.dynamic_slice_in_dim(rate_log, head_start, local_heads, 0)
    )
    allowed = visible(here_pos, group_pos, here_slide, group_slide, widths, strides)
    scores = (
        jnp.einsum("ihd,jhd->hij", query_heads, keys_all, preferred_element_type=jnp.float32)
        * scale
    )
    probability = softmax_rows(scores, allowed)
    rounded = probability.astype(jnp.bfloat16)
    slide_heads = (
        jnp.einsum("hij,jhd->ihd", rounded, values_all, preferred_element_type=jnp.float32)
        .astype(jnp.bfloat16)
        .reshape(row_count, head_cols)
    )
    upstream = out_grad.reshape(row_count, local_heads, HEAD_DIM)
    prob_grad = jnp.einsum("ihd,jhd->hij", upstream, values_all, preferred_element_type=jnp.float32)
    delta = jnp.sum(probability * prob_grad, axis=-1, keepdims=True)
    score_grad = (probability * (prob_grad - delta)).astype(jnp.bfloat16)
    query_grad = (
        jnp.einsum("hij,jhd->ihd", score_grad, keys_all, preferred_element_type=jnp.float32) * scale
    ).astype(jnp.bfloat16)
    key_part = (
        jnp.einsum("hij,ihd->jhd", score_grad, query_heads, preferred_element_type=jnp.float32)
        * scale
    )
    value_part = jnp.einsum("hij,ihd->jhd", rounded, upstream, preferred_element_type=jnp.float32)
    reduced = group_reduce(
        jnp.stack(
            [key_part.reshape(group_count, head_cols), value_part.reshape(group_count, head_cols)]
        ),
        seq_place,
    )
    key_grad = reduced[0].astype(jnp.bfloat16)
    value_grad = reduced[1].astype(jnp.bfloat16)
    local_grad = jnp.concatenate(
        [query_grad.reshape(row_count, head_cols), key_grad, value_grad], axis=1
    )
    returning = unpack(reroute(pack(local_grad, recv_slot)), send_slot)
    entering_grad = share_sum(
        lax.dot_general(
            returning, weight_flat, (((1,), (1,)), ((), ())), preferred_element_type=jnp.float32
        )
    )
    summed_grad, mixed_grad = tile_backward(
        entering_grad, saved_state, tile_gain, slide_proj, slide_gain, layer_scale
    )
    tile_grad = lax.dynamic_slice_in_dim(summed_grad, mp_place * share_rows, share_rows, 0).astype(
        jnp.bfloat16
    )
    head_grad = lax.dot_general(
        mixed_grad, out_proj, (((1,), (1,)), ((), ())), preferred_element_type=jnp.float32
    ).astype(jnp.bfloat16)
    return (slide_heads, tile_grad, head_grad)


def solution(mesh):
    in_specs = (
        P(("groups", "seq"), "mp"),
        P(("groups", "seq"), "mp"),
        P("mp", None),
        P(),
        P(),
        P(),
        P(),
        P(None, None, "mp"),
        P("groups"),
        P("groups"),
        P(),
        P(),
        P(("groups", "seq"), "mp"),
    )
    out_specs = (
        P(("groups", "seq"), "mp"),
        P(("groups", "seq", "mp"), None),
        P(("groups", "seq"), "mp"),
    )
    return jax.shard_map(shards, mesh=mesh, in_specs=in_specs, out_specs=out_specs, check_vma=False)
```

profile of v0, /device:TPU:0, one launch (start us, length us, event | category | flops | bytes accessed | tf_op | source)
XLA Modules:
  0.0 216.2 jit_solution(13706103607102826872)
XLA Ops:
  7.3 1.9 convolution_multiply_fusion
  9.3 1.0 copy-done.6
  10.4 0.2 convert_reduce_fusion.1
  10.6 3.4 %scatter_custom_fusion.1 = s32[768]{0:T(1024)S(1)} fusion(s32[768]{0:T(1024)S(1)} %compare_select_fusion, s32[768]{0:T(1024)S(1)} %iota.32, s32[]{:T(128)} %constant.100.clone.1), kind=kCustom, calls=%fused_computation.111 | custom fusion | bytes 3076 | tf_op jit(solution)/shard_map/scatter | solution.py:165
  14.1 0.7 fusion.46
  14.8 1.3 broadcast_compare_fusion.1
  16.1 1.2 scatter_custom_fusion
  17.3 0.6 iota_add_fusion.1
  17.9 0.6 pad_clamp_fusion.3
  18.5 0.8 convert_reduce_fusion
  19.3 31.1 %all-reduce.5.cloned.1.call-done = f32[192,1536]{1,0:T(8,128)} async-done(((f32[192,1536]{1,0:T(8,128)}), f32[192,1536]{1,0:T(8,128)}) %all-reduce.5.cloned.1.call-update) | async-done | bytes 1179664 | tf_op jit(solution)/shard_map/psum | solution.py:57
  50.4 1.5 reduce_sum.126
  52.0 0.3 multiply_reduce_fusion.1
  52.4 0.8 fusion.49
  53.2 0.2 multiply_reduce_fusion.3
  53.4 0.5 copy-done.3
  54.0 0.5 convolution_convert_fusion
  54.6 2.6 %gather_fusion = bf16[384,576]{1,0:T(8,128)(2,1)} fusion(bf16[193,576]{1,0:T(8,128)(2,1)S(1)} %concatenate.21, s32[1024]{0:T(1024)S(1)} %copy-done.32), kind=kCustom, calls=%fused_computation | custom fusion | bytes 886272 | tf_op jit(solution)/shard_map/gather | solution.py:181
  57.2 4.6 %all-to-all-start = ((bf16[4,96,576]{2,1,0:T(8,128)(2,1)}), bf16[4,96,576]{2,1,0:T(8,128)(2,1)S(1)}, u32[]{:S(2)}, u32[]{:S(2)}) async-start(bf16[4,96,576]{2,1,0:T(8,128)(2,1)} %bitcast.1), calls=%async_computation | async-start | bytes 983040 | tf_op jit(solution)/shard_map/all_to_all | solution.py:61
  61.9 1.2 add_select_fusion
  63.1 12.3 %all-to-all-done = bf16[4,96,576]{2,1,0:T(8,128)(2,1)S(1)} async-done(((bf16[4,96,576]{2,1,0:T(8,128)(2,1)}), bf16[4,96,576]{2,1,0:T(8,128)(2,1)S(1)}, u32[]{:S(2)}, u32[]{:S(2)}) %all-to-all-start) | async-done | bytes 442400 | tf_op jit(solution)/shard_map/all_to_all | solution.py:61
  75.4 1.0 gather_fusion.1
  76.7 0.9 add_select_fusion.1
  77.6 0.2 reduce-window.8
  77.7 1.6 copy.36
  79.4 1.8 scatter_custom_fusion.2
  81.2 1.3 collective-permute-done
  82.6 0.8 collective-permute-start.1
  83.5 0.8 broadcast_compare_fusion
  84.4 16.7 %collective-permute-done.1 = bf16[2,384,192]{2,1,0:T(8,128)(2,1)S(1)} collective-permute-done((bf16[2,384,192]{2,1,0:T(8,128)(2,1)S(1)}, bf16[2,384,192]{2,1,0:T(8,128)(2,1)S(1)}, u32[]{:S(2)}, u32[]{:S(2)}) %collective-permute-start.1) | collective-permute-done | bytes 294944 | tf_op jit(solution)/shard_map/ppermute | solution.py:20
  101.2 0.3 maximum_select_fusion
  101.5 0.2 copy.35
  101.7 0.2 copy.33
  101.9 3.3 %fusion.50 = (f32[3,192]{1,0:T(4,128)S(1)}, f32[3,192,768]{2,1,0:T(8,128)}) fusion(bf16[192,3,64]{0,2,1:T(8,128)(2,1)S(1)} %bitcast.72, bf16[768,3,64]{0,2,1:T(8,128)(2,1)S(1)} %bitcast.67, s32[3,768]{1,0:T(4,128)} %get-tuple-element.28, s32[3,192]{1,0:T(4,128)} %get-tuple-element.32, s32[3,768]{1,0:T(4,128)} %get-tuple-element.27, ...), kind=kOutput, calls=%fused_computation.142 | convolution fusion | flops 60162816 | bytes 2310912 | tf_op jit(solution)/shard_map/sub | solution.py:52
  105.3 3.3 %fusion.14 = f32[3,768,64]{1,2,0:T(8,128)} fusion(bf16[192,3,64]{0,2,1:T(8,128)(2,1)S(1)} %bitcast.79, f32[3,192]{1,0:T(4,128)S(1)} %get-tuple-element.35, bf16[192,3,64]{0,2,1:T(8,128)(2,1)S(1)} %bitcast.73, bf16[768,3,64]{0,2,1:T(8,128)(2,1)S(1)} %bitcast.68, s32[3,768]{1,0:T(4,128)S(1)} %copy-done.30, s32[3,192]{1,0:T(4,128)S(1)} %copy-done.41, ...), kind=kOutput, calls=%fused_computation.52 | convolution fusion | flops 117228864 | bytes 1204992 | tf_op jit(solution)/shard_map/hij,ihd->jhd/dot_general | solution.py:229
  108.6 2.2 fusion.1
  110.8 1.0 fusion.3
  111.8 1.1 convolution_multiply_fusion.2
  112.9 2.2 %copy.37 = f32[1,768,192]{2,1,0:T(8,128)} copy(f32[1,768,192]{1,2,0:T(8,128)} %bitcast.66) | data formatting | bytes 1179648 | tf_op jit(solution)/shard_map/stack;reshape | solution.py:231
  115.2 2.3 %copy.38 = f32[1,768,192]{2,1,0:T(8,128)} copy(f32[1,768,192]{1,2,0:T(8,128)} %bitcast.71) | data formatting | bytes 1179648 | tf_op jit(solution)/shard_map/stack;reshape | solution.py:231
  117.4 1.6 select_convert_fusion
  119.1 0.7 compare_select_fusion.1
  119.8 0.6 pad_clamp_fusion.1
  120.4 16.9 %collective-permute-done.2 = bf16[2,384,192]{2,1,0:T(8,128)(2,1)S(1)} collective-permute-done((bf16[2,384,192]{2,1,0:T(8,128)(2,1)S(1)}, bf16[2,384,192]{2,1,0:T(8,128)(2,1)S(1)}, u32[]{:S(2)}, u32[]{:S(2)}) %collective-permute-start.2) | collective-permute-done | bytes 294944 | tf_op jit(solution)/shard_map/ppermute | solution.py:20
  137.3 0.1 convert_add_fusion
  137.4 0.8 select_convert_fusion.1
  138.2 1.1 fusion.4
  139.3 1.0 copy.39
  140.3 5.1 %collective-permute-done.3 = bf16[2,192,192]{2,1,0:T(8,128)(2,1)} collective-permute-done((bf16[2,192,192]{2,1,0:T(8,128)(2,1)}, bf16[2,192,192]{2,1,0:T(8,128)(2,1)}, u32[]{:S(2)}, u32[]{:S(2)}) %collective-permute-start.3) | collective-permute-done | bytes 147488 | tf_op jit(solution)/shard_map/ppermute | solution.py:20
  145.3 1.3 add_convert_fusion
  146.8 2.8 %gather_fusion.2 = bf16[384,576]{1,0:T(8,128)(2,1)} fusion(bf16[193,576]{1,0:T(8,128)(2,1)S(1)} %fusion.26, s32[1024]{0:T(1024)} %pad_clamp_fusion.1), kind=kCustom, calls=%fused_computation.2 | custom fusion | bytes 886272 | tf_op jit(solution)/shard_map/gather | solution.py:181
  149.5 3.8 %all-to-all-start.1 = ((bf16[4,96,576]{2,1,0:T(8,128)(2,1)}), bf16[4,96,576]{2,1,0:T(8,128)(2,1)S(1)}, u32[]{:S(2)}, u32[]{:S(2)}) async-start(bf16[4,96,576]{2,1,0:T(8,128)(2,1)} %bitcast.22), calls=%async_computation.1 | async-start | bytes 983040 | tf_op jit(solution)/shard_map/all_to_all | solution.py:61
  153.3 13.1 %all-to-all-done.1 = bf16[4,96,576]{2,1,0:T(8,128)(2,1)S(1)} async-done(((bf16[4,96,576]{2,1,0:T(8,128)(2,1)}), bf16[4,96,576]{2,1,0:T(8,128)(2,1)S(1)}, u32[]{:S(2)}, u32[]{:S(2)}) %all-to-all-start.1) | async-done | bytes 442400 | tf_op jit(solution)/shard_map/all_to_all | solution.py:61
  166.5 1.0 gather_fusion.3
  167.5 2.4 %fusion.51 = f32[192,768]{1,0:T(8,128)} fusion(bf16[192,576]{1,0:T(8,128)(2,1)S(1)} %gather_fusion.3, bf16[768,576]{0,1:T(8,128)(2,1)} %bitcast.64), kind=kOutput, calls=%fused_computation.143 | convolution fusion | flops 169869312 | bytes 1695744 | tf_op jit(solution)/shard_map/dot_general | solution.py:243
  170.1 3.2 %convolution_convert_fusion.2 = bf16[3,64,192]{2,1,0:T(8,128)(2,1)} fusion(bf16[768,3,64]{0,2,1:T(8,128)(2,1)S(1)} %bitcast.78, f32[3,192]{1,0:T(4,128)S(1)} %copy-done.48, bf16[192,3,64]{0,2,1:T(8,128)(2,1)S(1)} %bitcast.75, bf16[768,3,64]{0,2,1:T(8,128)(2,1)S(1)} %bitcast.70, s32[3,768]{1,0:T(4,128)S(1)} %copy-done.31, s32[3,192]{1,0:T(4,128)S(1)} %copy-done.42, ...), kind=kOutput, calls=%fused_computation.28 | convolution fusion | flops 117265728 | bytes 910080 | tf_op jit(solution)/shard_map/hij,jhd->ihd/dot_general | solution.py:214
  173.3 1.7 copy.40
  175.0 27.2 %all-reduce.7.cloned.1.call-done = f32[192,768]{1,0:T(8,128)} async-done(((f32[192,768]{1,0:T(8,128)}), f32[192,768]{1,0:T(8,128)}) %all-reduce.7.cloned.1.call-update) | async-done | bytes 589840 | tf_op jit(solution)/shard_map/psum | solution.py:57
  202.2 1.5 multiply_reduce_fusion.4
  203.8 2.4 %fusion.45 = (f32[192]{0:T(256)S(1)}, f32[192]{0:T(256)S(1)}, f32[192,1536]{1,0:T(8,128)S(1)}) fusion(f32[192]{0:T(256)} %copy-done.26, f32[192,1536]{1,0:T(8,128)S(1)} %copy-done.2, f32[192]{0:T(256)} %copy-done.21, f32[1536]{0:T(1024)S(1)} %copy-done.19, bf16[1536,768]{1,0:T(8,128)(2,1)S(1)} %copy-done, f32[192,768]{1,0:T(8,128)} %all-reduce.7.cloned.1.call-done, ...), kind=kOutput, calls=%fused_computation.137 | convolution fusion | flops 455933568 | bytes 5913600 | tf_op jit(solution)/shard_map/dot_general | solution.py:107
  206.2 0.4 subtract_multiply_fusion
  206.7 0.8 copy-done.8
  207.5 1.2 convolution_convert_fusion.1
  208.7 0.7 dynamic-slice_convert_fusion
  (136 shorter events, 1.6 us)
Async XLA Ops:
  7.2 45.2 %copy-start = (bf16[1536,768]{1,0:T(8,128)(2,1)S(1)}, bf16[1536,768]{1,0:T(8,128)(2,1)}, u32[]{:S(2)}) copy-start(bf16[1536,768]{1,0:T(8,128)(2,1)} %param.18) | copy-start | bytes 7077892
  7.2 43.2 %all-reduce.5.cloned.1.call-start = ((), (), s32[]{:S(2)}) async-start(), calls=%async_computation.2 | async-start | bytes 2359296 | tf_op jit(solution)/shard_map/psum | solution.py:57
  7.2 1.9 copy-start.16
  7.2 3.1 %copy-start.34 = (s32[768]{0:T(1024)S(1)}, s32[768]{0:T(1024)}, u32[]{:S(2)}) copy-start(s32[768]{0:T(1024)} %param.21) | copy-start | bytes 9220
  7.3 6.9 %copy-start.49 = (s32[12]{0:T(128)S(1)}, s32[12]{0:T(128)}, u32[]{:S(2)}) copy-start(s32[12]{0:T(128)} %param.23) | copy-start | bytes 148
  9.2 1.0 copy-start.6
  9.2 43.1 %copy-start.19 = (f32[1536]{0:T(1024)S(1)}, f32[1536]{0:T(1024)}, u32[]{:S(2)}) copy-start(f32[1536]{0:T(1024)} %param.17) | copy-start | bytes 18436
  14.1 5.2 %copy-start.23 = (s32[192]{0:T(256)}, s32[192]{0:T(256)S(1)}, u32[]{:S(2)}) copy-start(s32[192]{0:T(256)S(1)} %get-tuple-element.29) | copy-start | bytes 2308
  14.1 5.2 %copy-start.45 = (s32[192]{0:T(256)}, s32[192]{0:T(256)S(1)}, u32[]{:S(2)}) copy-start(s32[192]{0:T(256)S(1)} %get-tuple-element.40) | copy-start | bytes 2308
  50.4 1.6 copy-start.1
  52.0 1.1 copy-start.21
  52.3 0.8 copy-start.26
  52.4 1.6 copy-start.9
  52.4 1.6 copy-start.18
  53.2 0.8 copy-start.3
  53.2 1.3 copy-start.32
  53.4 1.1 copy-start.25
  54.5 7.3 %copy-start.24 = (s32[192]{0:T(256)S(1)}, s32[192]{0:T(256)}, u32[]{:S(2)}) copy-start(s32[192]{0:T(256)} %copy-done.23) | copy-start | bytes 2308
  54.5 7.3 %copy-start.43 = (s32[192]{0:T(256)S(1)}, s32[192]{0:T(256)}, u32[]{:S(2)}) copy-start(s32[192]{0:T(256)} %convert_reduce_fusion) | copy-start | bytes 2308
  54.6 7.3 %copy-start.35 = (s32[3]{0:T(128)S(1)}, s32[3]{0:T(128)}, u32[]{:S(2)}) copy-start(s32[3]{0:T(128)} %get-tuple-element.16) | copy-start | bytes 40
  54.6 7.3 %copy-start.36 = (s32[3]{0:T(128)S(1)}, s32[3]{0:T(128)}, u32[]{:S(2)}) copy-start(s32[3]{0:T(128)} %get-tuple-element.17) | copy-start | bytes 40
  54.6 7.3 %copy-start.37 = (pred[3]{0:T(512)(128)(4,1)S(1)}, pred[3]{0:T(512)(128)(4,1)}, u32[]{:S(2)}) copy-start(pred[3]{0:T(512)(128)(4,1)} %get-tuple-element.18) | copy-start | bytes 13
  54.6 7.3 %copy-start.38 = (s32[3]{0:T(128)S(1)}, s32[3]{0:T(128)}, u32[]{:S(2)}) copy-start(s32[3]{0:T(128)} %get-tuple-element.19) | copy-start | bytes 40
  57.2 18.2 %all-to-all-start = ((bf16[4,96,576]{2,1,0:T(8,128)(2,1)}), bf16[4,96,576]{2,1,0:T(8,128)(2,1)S(1)}, u32[]{:S(2)}, u32[]{:S(2)}) async-start(bf16[4,96,576]{2,1,0:T(8,128)(2,1)} %bitcast.1), calls=%async_computation | async-start | bytes 983040 | tf_op jit(solution)/shard_map/all_to_all | solution.py:61
  61.8 14.8 %copy-start.33 = (s32[192]{0:T(256)S(1)}, s32[192]{0:T(256)}, u32[]{:S(2)}) copy-start(s32[192]{0:T(256)} %get-tuple-element.41) | copy-start | bytes 2308
  61.8 14.9 %copy-start.44 = (s32[192]{0:T(256)S(1)}, s32[192]{0:T(256)}, u32[]{:S(2)}) copy-start(s32[192]{0:T(256)} %get-tuple-element.42) | copy-start | bytes 2308
  61.8 15.7 %copy-start.50 = (s32[4]{0:T(128)S(1)}, s32[4]{0:T(128)}, u32[]{:S(2)}) copy-start(s32[4]{0:T(128)} %param.22) | copy-start | bytes 52
  76.6 5.9 %collective-permute-start = (bf16[2,192,192]{2,1,0:T(8,128)(2,1)S(1)}, bf16[2,192,192]{2,1,0:T(8,128)(2,1)S(1)}, u32[]{:S(2)}, u32[]{:S(2)}) collective-permute-start(bf16[2,192,192]{2,1,0:T(8,128)(2,1)S(1)} %pad_maximum_fusion.1), channel_id=1, source_target_pairs={{0,4},{4,0},{8,12},{12,8},{1,5},{5,1},{9,13},{13,9},{2,6},{6,2},{1... | collective-permute-start | bytes 442376 | tf_op jit(solution)/shard_map/ppermute | solution.py:20
  82.6 18.5 %collective-permute-start.1 = (bf16[2,384,192]{2,1,0:T(8,128)(2,1)S(1)}, bf16[2,384,192]{2,1,0:T(8,128)(2,1)S(1)}, u32[]{:S(2)}, u32[]{:S(2)}) collective-permute-start(bf16[2,384,192]{2,1,0:T(8,128)(2,1)S(1)} %maximum_select_fusion.1), channel_id=1, source_target_pairs={{0,8},{8,0},{4,12},{12,4},{1,9},{9,1},{5,13},{13,5},{2,10},{10,2},... | collective-permute-start | bytes 884744 | tf_op jit(solution)/shard_map/ppermute | solution.py:20
  84.4 20.8 %copy-start.11 = (bf16[192,192]{0,1:T(8,128)(2,1)}, bf16[192,192]{0,1:T(8,128)(2,1)S(1)}, u32[]{:S(2)}) copy-start(bf16[192,192]{0,1:T(8,128)(2,1)S(1)} %copy.34) | copy-start | bytes 221188
  101.9 6.7 %copy-start.14 = (bf16[1,768,192]{1,2,0:T(8,128)(2,1)}, bf16[1,768,192]{1,2,0:T(8,128)(2,1)S(1)}, u32[]{:S(2)}) copy-start(bf16[1,768,192]{1,2,0:T(8,128)(2,1)S(1)} %copy.33) | copy-start | bytes 884740
  101.9 3.4 %copy-start.17 = (bf16[192,192]{0,1:T(8,128)(2,1)S(1)}, bf16[192,192]{0,1:T(8,128)(2,1)}, u32[]{:S(2)}) copy-start(bf16[192,192]{0,1:T(8,128)(2,1)} %copy.36) | copy-start | bytes 221188
  101.9 3.4 %copy-start.28 = (s32[3,768]{1,0:T(4,128)S(1)}, s32[3,768]{1,0:T(4,128)}, u32[]{:S(2)}) copy-start(s32[3,768]{1,0:T(4,128)} %get-tuple-element.27) | copy-start | bytes 27652
  101.9 3.4 %copy-start.30 = (s32[3,768]{1,0:T(4,128)S(1)}, s32[3,768]{1,0:T(4,128)}, u32[]{:S(2)}) copy-start(s32[3,768]{1,0:T(4,128)} %get-tuple-element.28) | copy-start | bytes 27652
  101.9 3.4 %copy-start.39 = (s32[3,192]{1,0:T(4,128)S(1)}, s32[3,192]{1,0:T(4,128)}, u32[]{:S(2)}) copy-start(s32[3,192]{1,0:T(4,128)} %get-tuple-element.31) | copy-start | bytes 6916
  101.9 3.4 %copy-start.41 = (s32[3,192]{1,0:T(4,128)S(1)}, s32[3,192]{1,0:T(4,128)}, u32[]{:S(2)}) copy-start(s32[3,192]{1,0:T(4,128)} %get-tuple-element.32) | copy-start | bytes 6916
  105.3 3.3 %copy-start.47 = (f32[3,192]{1,0:T(4,128)}, f32[3,192]{1,0:T(4,128)S(1)}, u32[]{:S(2)}) copy-start(f32[3,192]{1,0:T(4,128)S(1)} %get-tuple-element.35) | copy-start | bytes 6916
  108.6 2.2 copy-start.10
  110.8 1.0 copy-start.12
  117.4 19.8 %copy-start.4 = (f32[1,768,192]{2,1,0:T(8,128)S(1)}, f32[1,768,192]{2,1,0:T(8,128)}, u32[]{:S(2)}) copy-start(f32[1,768,192]{2,1,0:T(8,128)} %copy.37) | copy-start | bytes 1769476
  117.4 19.8 %copy-start.5 = (f32[1,768,192]{2,1,0:T(8,128)S(1)}, f32[1,768,192]{2,1,0:T(8,128)}, u32[]{:S(2)}) copy-start(f32[1,768,192]{2,1,0:T(8,128)} %copy.38) | copy-start | bytes 1769476
  119.0 18.2 %collective-permute-start.2 = (bf16[2,384,192]{2,1,0:T(8,128)(2,1)S(1)}, bf16[2,384,192]{2,1,0:T(8,128)(2,1)S(1)}, u32[]{:S(2)}, u32[]{:S(2)}) collective-permute-start(bf16[2,384,192]{2,1,0:T(8,128)(2,1)S(1)} %select_convert_fusion), channel_id=1, source_target_pairs={{0,8},{8,0},{4,12},{12,4},{1,9},{9,1},{5,13},{13,5},{2,10},{10,2},... | collective-permute-start | bytes 884744 | tf_op jit(solution)/shard_map/ppermute | solution.py:20
  137.4 1.9 copy-start.7
  138.2 7.1 %collective-permute-start.3 = (bf16[2,192,192]{2,1,0:T(8,128)(2,1)}, bf16[2,192,192]{2,1,0:T(8,128)(2,1)}, u32[]{:S(2)}, u32[]{:S(2)}) collective-permute-start(bf16[2,192,192]{2,1,0:T(8,128)(2,1)} %select_convert_fusion.1), channel_id=1, source_target_pairs={{0,4},{4,0},{8,12},{12,8},{1,5},{5,1},{9,13},{13,9},{2,6},{6,2},{1... | collective-permute-start | bytes 442376 | tf_op jit(solution)/shard_map/ppermute | solution.py:20
  146.8 6.6 %copy-start.46 = (s32[192]{0:T(256)S(1)}, s32[192]{0:T(256)}, u32[]{:S(2)}) copy-start(s32[192]{0:T(256)} %copy-done.45) | copy-start | bytes 2308
  149.5 16.9 %all-to-all-start.1 = ((bf16[4,96,576]{2,1,0:T(8,128)(2,1)}), bf16[4,96,576]{2,1,0:T(8,128)(2,1)S(1)}, u32[]{:S(2)}, u32[]{:S(2)}) async-start(bf16[4,96,576]{2,1,0:T(8,128)(2,1)} %bitcast.22), calls=%async_computation.1 | async-start | bytes 983040 | tf_op jit(solution)/shard_map/all_to_all | solution.py:61
  153.3 48.9 %all-reduce.7.cloned.1.call-start = ((), (), s32[]{:S(2)}) async-start(), calls=%async_computation.3 | async-start | bytes 1179648 | tf_op jit(solution)/shard_map/psum | solution.py:57
  166.5 3.6 %copy-start.13 = (bf16[192,192]{0,1:T(8,128)(2,1)S(1)}, bf16[192,192]{0,1:T(8,128)(2,1)}, u32[]{:S(2)}) copy-start(bf16[192,192]{0,1:T(8,128)(2,1)} %copy-done.11) | copy-start | bytes 221188
  166.5 3.6 %copy-start.29 = (s32[3,768]{1,0:T(4,128)S(1)}, s32[3,768]{1,0:T(4,128)}, u32[]{:S(2)}) copy-start(s32[3,768]{1,0:T(4,128)} %get-tuple-element.27) | copy-start | bytes 27652
  166.5 3.6 %copy-start.31 = (s32[3,768]{1,0:T(4,128)S(1)}, s32[3,768]{1,0:T(4,128)}, u32[]{:S(2)}) copy-start(s32[3,768]{1,0:T(4,128)} %get-tuple-element.28) | copy-start | bytes 27652
  166.5 3.6 %copy-start.40 = (s32[3,192]{1,0:T(4,128)S(1)}, s32[3,192]{1,0:T(4,128)}, u32[]{:S(2)}) copy-start(s32[3,192]{1,0:T(4,128)} %get-tuple-element.31) | copy-start | bytes 6916
  166.5 3.6 %copy-start.42 = (s32[3,192]{1,0:T(4,128)S(1)}, s32[3,192]{1,0:T(4,128)}, u32[]{:S(2)}) copy-start(s32[3,192]{1,0:T(4,128)} %get-tuple-element.32) | copy-start | bytes 6916
  166.5 3.6 %copy-start.48 = (f32[3,192]{1,0:T(4,128)S(1)}, f32[3,192]{1,0:T(4,128)}, u32[]{:S(2)}) copy-start(f32[3,192]{1,0:T(4,128)} %copy-done.47) | copy-start | bytes 6916
  167.5 2.5 %copy-start.15 = (bf16[1,768,192]{1,2,0:T(8,128)(2,1)S(1)}, bf16[1,768,192]{1,2,0:T(8,128)(2,1)}, u32[]{:S(2)}) copy-start(bf16[1,768,192]{1,2,0:T(8,128)(2,1)} %copy-done.14) | copy-start | bytes 884740
  173.3 30.4 %copy-start.2 = (f32[192,1536]{1,0:T(8,128)S(1)}, f32[192,1536]{1,0:T(8,128)}, u32[]{:S(2)}) copy-start(f32[192,1536]{1,0:T(8,128)} %all-reduce.5.cloned.1.call-done) | copy-start | bytes 3538948
  203.7 2.4 %copy-start.22 = (f32[192]{0:T(256)S(1)}, f32[192]{0:T(256)}, u32[]{:S(2)}) copy-start(f32[192]{0:T(256)} %copy-done.21) | copy-start | bytes 2308
  203.8 2.4 %copy-start.27 = (f32[192]{0:T(256)S(1)}, f32[192]{0:T(256)}, u32[]{:S(2)}) copy-start(f32[192]{0:T(256)} %copy-done.26) | copy-start | bytes 2308
  206.2 1.3 copy-start.8
  206.2 1.3 copy-start.20
Sparse Core Ops, SparseCore 0:
  10.4 39.9 all-reduce.4
  170.1 32.0 all-reduce.6
where the time goes:
time: 217 us; the launch traced here: 216 us
  waiting for transfers between devices  124 us (57%)
  local copies, waits for them, and re-layouts  26.7 us (12%)
  matrix products  23.3 us (11%)
  other arithmetic  18.2 us (8%)
  between operations  14.9 us (7%)
  starting transfers between devices  9.36 us (4%)
    psum x2, waiting for transfers between devices, share_sum(): return lax.psum(values, 'mp')  58.3 us
    ppermute x4, waiting for transfers between devices, swapped(): return lax.ppermute(block, axis, route)  40 us
    all_to_all x2, waiting for transfers between devices, reroute(): lax.all_to_all(buffer, 'seq', split_axis=0, concat_axis=0, tiled=True)  25.4 us
    all_to_all x2, starting transfers between devices, reroute(): lax.all_to_all(buffer, 'seq', split_axis=0, concat_axis=0, tiled=True)  8.39 us
    unnamed x104, local copies, waits for them, and re-layouts  6.09 us
    gather x2, local copies, waits for them, and re-layouts, pack(): return padded[slot_table].reshape(seq_count, capacity, values.shape[1])  5.39 us
    another operation x2, local copies, waits for them, and re-layouts, shards(): jnp.stack([key_part.reshape(group_count, head_cols), value_part.reshape(g...  4.51 us
  transfers between devices with their start and end apart: 8, of which 8 were waited for; matrix products, arithmetic and copies ran while one was open for 11% of the time, Pallas kernels for 0%

commit v1 on v0

--- a/solution.py
+++ b/solution.py
@@ -1,6 +1,8 @@
 import jax
 import jax.numpy as jnp
 from jax import lax
+from jax.experimental import pallas as pl
+from jax.experimental.pallas import tpu as pltpu
 from jax.sharding import PartitionSpec as P
 
 HEAD_DIM = 64
@@ -8,6 +10,7 @@
 
 
 EPSILON = 1e-06
+SCALE = HEAD_DIM ** (-0.5)
 
 
 def swapped(block, axis, distance):
@@ -256,7 +259,500 @@
     return (slide_heads, tile_grad, head_grad)
 
 
+F32 = jnp.float32
+BF16 = jnp.bfloat16
+MESH = pl.DeviceIdType.MESH
+HIDDEN = -1e30
+GROUP_SEQ = 1 << SPAN_LOG
+QUAD = 4
+
+
+def rows_dot(left, right):
+    return lax.dot_general(left, right, (((1,), (1,)), ((), ())), preferred_element_type=F32)
+
+
+def cols_dot(left, right):
+    return lax.dot_general(left, right, (((0,), (0,)), ((), ())), preferred_element_type=F32)
+
+
+def plain_dot(left, right):
+    return jnp.dot(left, right, preferred_element_type=F32)
+
+
+def step_kernel(
+    features_ref,
+    outputs_ref,
+    out_proj_ref,
+    layer_scale_ref,
+    tile_gain_ref,
+    slide_proj_hbm,
+    slide_gain_ref,
+    weight_hbm,
+    slot_ref,
+    len_ref,
+    seg_ref,
+    rate_ref,
+    grad_ref,
+    heads_out,
+    tile_out,
+    head_out,
+    slide_proj_ref,
+    weight_ref,
+    upstream_all,
+    term_ref,
+    first_out,
+    first_in,
+    second_out,
+    second_in,
+    entering_all,
+    query_ref,
+    key_ref,
+    value_ref,
+    upstream_ref,
+    bias_row,
+    bias_col,
+    score_buf,
+    grad_buf,
+    stats_pad,
+    stats_all,
+    heads_all,
+    back_ref,
+    back_first_out,
+    back_first_in,
+    back_second_out,
+    back_second_in,
+    mixed_all,
+    load_sem,
+    up_send,
+    up_recv,
+    scatter_send,
+    scatter_recv,
+    z_send,
+    z_recv,
+    x_send,
+    x_recv,
+    core_send,
+    core_recv,
+    stats_send,
+    stats_recv,
+    heads_send,
+    heads_recv,
+    back_send,
+    back_recv,
+    mixed_send,
+    mixed_recv,
+):
+    rows, width_part = features_ref.shape
+    total = GROUP_SEQ * rows
+    share = rows // QUAD
+    head_cols = grad_ref.shape[1]
+    local_heads = head_cols // HEAD_DIM
+    seq = lax.axis_index("seq")
+    mp = lax.axis_index("mp")
+    sibling = mp + 1 - 2 * (mp % 2)
+    across = (mp + 2) % QUAD
+    corner = (sibling + 2) % QUAD
+
+    def remote(source, target, send, recv, where):
+        return pltpu.make_async_remote_copy(
+            src_ref=source,
+            dst_ref=target,
+            send_sem=send,
+            recv_sem=recv,
+            device_id=where,
+            device_id_type=MESH,
+        )
+
+    slide_load = pltpu.make_async_copy(slide_proj_hbm, slide_proj_ref, load_sem.at[0])
+    weight_load = pltpu.make_async_copy(weight_hbm, weight_ref, load_sem.at[1])
+    slide_load.start()
+    weight_load.start()
+
+    barrier = pltpu.get_barrier_semaphore()
+    for offset in range(1, GROUP_SEQ):
+        pl.semaphore_signal(
+            barrier, inc=1, device_id={"seq": (seq + offset) % GROUP_SEQ}, device_id_type=MESH
+        )
+    for offset in range(1, QUAD):
+        pl.semaphore_signal(
+            barrier, inc=1, device_id={"mp": (mp + offset) % QUAD}, device_id_type=MESH
+        )
+
+    term_ref[...] = layer_scale_ref[...] * plain_dot(outputs_ref[...], out_proj_ref[...])
+    own_cols = pl.ds(pl.multiple_of(mp * width_part, 128), width_part)
+    term_ref[:, own_cols] += features_ref[...].astype(F32)
+
+    def share_of(place):
+        return pl.ds(pl.multiple_of(place * share, 16), share)
+
+    pl.semaphore_wait(barrier, GROUP_SEQ - 1 + QUAD - 1)
+
+    def scatter_first(source, out_buf, in_buf, send, recv):
+        copies = []
+        for slot, place in ((1, corner), (0, sibling)):
+            out_buf[slot] = source[share_of(place), :].astype(BF16)
+            copy = remote(
+                out_buf.at[slot], in_buf.at[slot], send.at[slot], recv.at[slot], {"mp": sibling}
+            )
+            copy.start()
+            copies.append(copy)
+        return copies
+
+    def scatter_second(source, copies, in_buf, out_ref, in_ref, send, recv):
+        copies[0].wait_recv()
+        out_ref[...] = (source[share_of(across), :] + in_buf[1].astype(F32)).astype(BF16)
+        copy = remote(out_ref, in_ref, send.at[2], recv.at[2], {"mp": across})
+        copy.start()
+        copies[1].wait_recv()
+        partial = source[share_of(mp), :] + in_buf[0].astype(F32)
+        copy.wait_recv()
+        for each in copies + [copy]:
+            each.wait_send()
+        return partial + in_ref[...].astype(F32)
+
+    first = scatter_first(term_ref, first_out, first_in, scatter_send, scatter_recv)
+
+    upstream_all[seq] = grad_ref[...]
+    up_copies = []
+    for offset in range(1, GROUP_SEQ):
+        copy = remote(
+            grad_ref,
+            upstream_all.at[seq],
+            up_send.at[offset - 1],
+            up_recv.at[offset - 1],
+            {"seq": (seq + offset) % GROUP_SEQ},
+        )
+        copy.start()
+        up_copies.append(copy)
+
+    slots = slot_ref[...]
+    base = seq * rows
+    bounds = []
+    reached = 0
+    for index in range(len_ref.shape[0]):
+        reached = reached + len_ref[index]
+        bounds.append(reached)
+    slide_of = jnp.zeros_like(slots)
+    for bound in bounds:
+        slide_of = slide_of + (slots >= bound).astype(jnp.int32)
+    window_of = jnp.zeros_like(slots)
+    for index in range(1, GROUP_SEQ):
+        window_of = window_of + (slots >= index * rows).astype(jnp.int32)
+    lane_all = lax.broadcasted_iota(jnp.int32, (rows, total), 1)
+    sub_all = lax.broadcasted_iota(jnp.int32, (rows, total), 0)
+    pick_own = (lane_all == sub_all + base).astype(BF16)
+    eye = (
+        lax.broadcasted_iota(jnp.int32, (total, total), 0)
+        == lax.broadcasted_iota(jnp.int32, (total, total), 1)
+    ).astype(BF16)
+    for head in range(local_heads):
+        seg = seg_ref[mp * local_heads + head]
+        rate = rate_ref[mp * local_heads + head]
+        stride_mask = jnp.left_shift(jnp.int32(1), rate) - 1
+        code = (
+            slide_of * (GROUP_SEQ * GROUP_SEQ)
+            + jnp.right_shift(window_of, jnp.full_like(window_of, seg)) * GROUP_SEQ
+            + (slots & stride_mask)
+        )
+        code_rows = jnp.broadcast_to(code.astype(F32), (rows, total))
+        code_bf = code_rows.astype(BF16)
+        code_own_lane = rows_dot(code_bf, pick_own)
+        code_all_sub = rows_dot(eye, code_bf)
+        bias_row[head] = jnp.where(code_all_sub == code_own_lane[:1], 0.0, HIDDEN)
+        code_own_sub = rows_dot(pick_own, code_bf)
+        bias_col[head] = jnp.where(code_own_sub[:, :1] == code_rows, 0.0, HIDDEN)
+    slot_rows = jnp.broadcast_to(slots, (rows, total))
+    pick_heads = (slot_rows == sub_all + base).astype(BF16)
+    arrange = (
+        jnp.broadcast_to(slots, (total, total)) == lax.broadcasted_iota(jnp.int32, (total, total), 0)
+    ).astype(BF16)
+
+    summed = scatter_second(
+        term_ref, first, first_in, second_out, second_in, scatter_send, scatter_recv
+    )
+    tile_normed, tile_inverse = norm_parts(summed)
+    lifted = (tile_normed * tile_gain_ref[...]).astype(BF16)
+    slide_load.wait()
+    embedded = plain_dot(lifted, slide_proj_ref[...])
+    slide_normed, slide_inverse = norm_parts(embedded)
+    entering_all[seq, mp] = (slide_normed * slide_gain_ref[...]).astype(BF16)
+
+    pending = []
+
+    def forward(source_seq, source_mp, send, recv, where):
+        copy = remote(
+            entering_all.at[source_seq, source_mp],
+            entering_all.at[source_seq, source_mp],
+            send,
+            recv,
+            where,
+        )
+        copy.start()
+        pending.append(copy)
+        return copy
+
+    z_copies = []
+    for offset in range(1, GROUP_SEQ):
+        z_copies.append(
+            forward(
+                seq,
+                mp,
+                z_send.at[offset - 1],
+                z_recv.at[offset - 1],
+                {"seq": (seq + offset) % GROUP_SEQ},
+            )
+        )
+    x_copies = [forward(seq, mp, x_send.at[0], x_recv.at[0], {"mp": across})]
+    core_copies = [forward(seq, mp, core_send.at[0], core_recv.at[0], {"mp": sibling})]
+
+    for copy in up_copies:
+        copy.wait()
+    upstream_ref[...] = cols_dot(arrange, upstream_all[...].reshape(total, head_cols)).astype(BF16)
+
+    for offset in range(1, GROUP_SEQ):
+        origin = (seq + GROUP_SEQ - offset) % GROUP_SEQ
+        z_copies[offset - 1].wait_recv()
+        x_copies.append(forward(origin, mp, x_send.at[offset], x_recv.at[offset], {"mp": across}))
+        core_copies.append(
+            forward(origin, mp, core_send.at[offset], core_recv.at[offset], {"mp": sibling})
+        )
+    for offset in range(GROUP_SEQ):
+        origin = (seq + GROUP_SEQ - offset) % GROUP_SEQ
+        x_copies[offset].wait_recv()
+        core_copies.append(
+            forward(
+                origin,
+                across,
+                core_send.at[GROUP_SEQ + offset],
+                core_recv.at[GROUP_SEQ + offset],
+                {"mp": sibling},
+            )
+        )
+    weight_load.wait()
+    for copy in core_copies:
+        copy.wait_recv()
+    entering = entering_all[...].reshape(total, entering_all.shape[3])
+    query_ref[...] = (rows_dot(entering, weight_ref[0]).astype(BF16).astype(F32) * SCALE).astype(
+        BF16
+    )
+    key_ref[...] = rows_dot(entering, weight_ref[1]).astype(BF16)
+    value_ref[...] = rows_dot(entering, weight_ref[2]).astype(BF16)
+    for copy in pending:
+        copy.wait_send()
+
+    own_rows = pl.ds(pl.multiple_of(base, 64), rows)
+
+    def head_only(values, head):
+        lane_head = lax.broadcasted_iota(jnp.int32, values.shape, 1) // HEAD_DIM
+        return jnp.where(lane_head == head, values, jnp.zeros_like(values))
+
+    stats_pad[...] = jnp.zeros_like(stats_pad)
+    heads_sum = jnp.zeros((rows, head_cols), F32)
+    query_sum = jnp.zeros((rows, head_cols), F32)
+    keys = key_ref[...]
+    values = value_ref[...]
+    for head in range(local_heads):
+        scores = rows_dot(keys, head_only(query_ref[own_rows, :], head)) + bias_row[head]
+        row_max = jnp.max(scores, axis=0, keepdims=True)
+        raised = jnp.exp(scores - row_max)
+        row_sum = jnp.sum(raised, axis=0, keepdims=True)
+        probability = raised * (1.0 / row_sum)
+        prob_grad = rows_dot(values, head_only(upstream_ref[own_rows, :], head))
+        delta = jnp.sum(probability * prob_grad, axis=0, keepdims=True)
+        stats_pad[2 * head : 2 * head + 1, :rows] = row_max + jnp.log(row_sum)
+        stats_pad[2 * head + 1 : 2 * head + 2, :rows] = delta
+        score_grad = (probability * (prob_grad - delta)).astype(BF16)
+        heads_sum = heads_sum + cols_dot(probability.astype(BF16), head_only(values, head))
+        query_sum = query_sum + cols_dot(score_grad, head_only(keys, head))
+    stats_all[seq] = pltpu.roll(stats_pad[...], base, 1)
+    heads_all[seq] = heads_sum.astype(BF16)
+    stats_copies = []
+    heads_copies = []
+    for offset in range(1, GROUP_SEQ):
+        copy = remote(
+            stats_all.at[seq],
+            stats_all.at[seq],
+            stats_send.at[offset - 1],
+            stats_recv.at[offset - 1],
+            {"seq": (seq + offset) % GROUP_SEQ},
+        )
+        copy.start()
+        stats_copies.append(copy)
+    for offset in range(1, GROUP_SEQ):
+        copy = remote(
+            heads_all.at[seq],
+            heads_all.at[seq],
+            heads_send.at[offset - 1],
+            heads_recv.at[offset - 1],
+            {"seq": (seq + offset) % GROUP_SEQ},
+        )
+        copy.start()
+        heads_copies.append(copy)
+    own_keys = key_ref[own_rows, :]
+    own_values = value_ref[own_rows, :]
+    queries = query_ref[...]
+    upstream = upstream_ref[...]
+    for head in range(local_heads):
+        score_buf[head] = rows_dot(own_keys, head_only(queries, head)) + bias_col[head]
+        grad_buf[head] = rows_dot(own_values, head_only(upstream, head))
+    for copy in stats_copies:
+        copy.wait()
+    stats = stats_all[0] + stats_all[1] + stats_all[2] + stats_all[3]
+    key_sum = jnp.zeros((rows, head_cols), F32)
+    value_sum = jnp.zeros((rows, head_cols), F32)
+    for head in range(local_heads):
+        probability = jnp.exp(score_buf[head] - stats[2 * head : 2 * head + 1])
+        score_grad = probability * (grad_buf[head] - stats[2 * head + 1 : 2 * head + 2])
+        value_sum = value_sum + plain_dot(probability.astype(BF16), head_only(upstream, head))
+        key_sum = key_sum + plain_dot(score_grad.astype(BF16), head_only(queries, head))
+    back_ref[...] = (
+        plain_dot((query_sum * SCALE).astype(BF16), weight_ref[0])
+        + plain_dot(key_sum.astype(BF16), weight_ref[1])
+        + plain_dot(value_sum.astype(BF16), weight_ref[2])
+    )
+    back_first = scatter_first(back_ref, back_first_out, back_first_in, back_send, back_recv)
+    entering_grad = scatter_second(
+        back_ref, back_first, back_first_in, back_second_out, back_second_in, back_send, back_recv
+    )
+    embedded_grad = norm_back(
+        entering_grad * slide_gain_ref[...], slide_normed, slide_inverse
+    ).astype(BF16)
+    lifted_grad = rows_dot(embedded_grad, slide_proj_ref[...])
+    summed_grad = norm_back(lifted_grad * tile_gain_ref[...], tile_normed, tile_inverse)
+    mixed_all[mp] = (layer_scale_ref[...] * summed_grad).astype(BF16)
+
+    def mixed_move(place, index, where):
+        copy = remote(
+            mixed_all.at[place],
+            mixed_all.at[place],
+            mixed_send.at[index],
+            mixed_recv.at[index],
+            {"mp": where},
+        )
+        copy.start()
+        return copy
+
+    mixed_x = mixed_move(mp, 0, across)
+    mixed_core = mixed_move(mp, 1, sibling)
+    tile_out[...] = summed_grad.astype(BF16)
+    for copy in heads_copies:
+        copy.wait()
+    heads_out[...] = plain_dot(pick_heads, heads_all[...].reshape(total, head_cols)).astype(BF16)
+    mixed_x.wait()
+    mixed_corner = mixed_move(across, 2, sibling)
+    mixed_core.wait()
+    mixed_corner.wait()
+    head_out[...] = rows_dot(
+        mixed_all[...].reshape(rows, mixed_all.shape[2]), out_proj_ref[...]
+    ).astype(BF16)
+
+
+def fused_shards(
+    tile_features,
+    head_outputs,
+    out_proj,
+    layer_scale,
+    tile_gain,
+    slide_proj,
+    slide_gain,
+    qkv_weight,
+    slide_slot,
+    slide_len,
+    seg_log,
+    rate_log,
+    out_grad,
+):
+    rows, width_part = tile_features.shape
+    width = out_proj.shape[1]
+    slide_width = slide_proj.shape[1]
+    head_cols = qkv_weight.shape[2]
+    local_heads = head_cols // HEAD_DIM
+    share = rows // QUAD
+    total = GROUP_SEQ * rows
+    vmem = pl.BlockSpec(memory_space=pltpu.VMEM)
+    smem = pl.BlockSpec(memory_space=pltpu.SMEM)
+    hbm = pl.BlockSpec(memory_space=pl.ANY)
+    dma = pltpu.SemaphoreType.DMA
+    return pl.pallas_call(
+        step_kernel,
+        out_shape=(
+            jax.ShapeDtypeStruct((rows, head_cols), BF16),
+            jax.ShapeDtypeStruct((share, width), BF16),
+            jax.ShapeDtypeStruct((rows, width_part), BF16),
+        ),
+        in_specs=[vmem, vmem, vmem, vmem, vmem, hbm, vmem, hbm, vmem, smem, smem, smem, vmem],
+        out_specs=(vmem, vmem, vmem),
+        scratch_shapes=[
+            pltpu.VMEM((width, slide_width), BF16),
+            pltpu.VMEM((3, head_cols, slide_width), BF16),
+            pltpu.VMEM((GROUP_SEQ, rows, head_cols), BF16),
+            pltpu.VMEM((rows, width), F32),
+            pltpu.VMEM((2, share, width), BF16),
+            pltpu.VMEM((2, share, width), BF16),
+            pltpu.VMEM((share, width), BF16),
+            pltpu.VMEM((share, width), BF16),
+            pltpu.VMEM((GROUP_SEQ, QUAD, share, slide_width), BF16),
+            pltpu.VMEM((total, head_cols), BF16),
+            pltpu.VMEM((total, head_cols), BF16),
+            pltpu.VMEM((total, head_cols), BF16),
+            pltpu.VMEM((total, head_cols), BF16),
+            pltpu.VMEM((local_heads, total, rows), F32),
+            pltpu.VMEM((local_heads, rows, total), F32),
+            pltpu.VMEM((local_heads, rows, total), F32),
+            pltpu.VMEM((local_heads, rows, total), F32),
+            pltpu.VMEM((8, total), F32),
+            pltpu.VMEM((GROUP_SEQ, 8, total), F32),
+            pltpu.VMEM((GROUP_SEQ, rows, head_cols), BF16),
+            pltpu.VMEM((rows, slide_width), F32),
+            pltpu.VMEM((2, share, slide_width), BF16),
+            pltpu.VMEM((2, share, slide_width), BF16),
+            pltpu.VMEM((share, slide_width), BF16),
+            pltpu.VMEM((share, slide_width), BF16),
+            pltpu.VMEM((QUAD, share, width), BF16),
+            dma((2,)),
+            dma((3,)),
+            dma((3,)),
+            dma((3,)),
+            dma((3,)),
+            dma((3,)),
+            dma((3,)),
+            dma((4,)),
+            dma((4,)),
+            dma((8,)),
+            dma((8,)),
+            dma((3,)),
+            dma((3,)),
+            dma((3,)),
+            dma((3,)),
+            dma((3,)),
+            dma((3,)),
+            dma((3,)),
+            dma((3,)),
+        ],
+        compiler_params=pltpu.CompilerParams(
+            collective_id=0, has_side_effects=True, vmem_limit_bytes=48 * 1024 * 1024
+        ),
+        name="slide_step",
+    )(
+        tile_features,
+        head_outputs,
+        out_proj,
+        layer_scale.reshape(1, width),
+        tile_gain.reshape(1, width),
+        slide_proj,
+        slide_gain.reshape(1, slide_width),
+        jnp.transpose(qkv_weight, (1, 2, 0)),
+        slide_slot.reshape(1, total),
+        slide_len,
+        seg_log,
+        rate_log,
+        out_grad,
+    )
+
+
 def solution(mesh):
+    fused = mesh.shape["seq"] == GROUP_SEQ and mesh.shape["mp"] == QUAD
+    body = fused_shards if fused else shards
     in_specs = (
         P(("groups", "seq"), "mp"),
         P(("groups", "seq"), "mp"),
@@ -277,4 +773,4 @@
         P(("groups", "seq", "mp"), None),
         P(("groups", "seq"), "mp"),
     )
-    return jax.shard_map(shards, mesh=mesh, in_specs=in_specs, out_specs=out_specs, check_vma=False)
+    return jax.shard_map(body, mesh=mesh, in_specs=in_specs, out_specs=out_specs, check_vma=False)

time: 217 us -> 63.8 us (0.29)
  waiting for transfers between devices: 124 us -> 0 us
  Pallas kernels: 0 us -> 48.4 us
  matrix products: 23.3 us -> 0 us
  other arithmetic: 18.2 us -> 0 us
  between operations: 14.9 us -> 0.65 us
  local copies, waits for them, and re-layouts: 26.7 us -> 13.5 us
  starting transfers between devices: 9.36 us -> 0 us
    psum x2 -> x0, waiting for transfers between devices: 58.3 us -> none  [share_sum(): return lax.psum(values, 'mp')]
    pallas_call x0 -> x1, Pallas kernels: none -> 48.4 us  [fused_shards(): pl.pallas_call(step_kernel, out_shape=(jax.ShapeDtypeStruct((rows, head_c...]
    ppermute x4 -> x0, waiting for transfers between devices: 40 us -> none  [swapped(): return lax.ppermute(block, axis, route)]
    all_to_all x2 -> x0, waiting for transfers between devices: 25.4 us -> none  [reroute(): lax.all_to_all(buffer, 'seq', split_axis=0, concat_axis=0, tiled=True)]
    dot_general x11 -> x0, matrix products: 20 us -> none  [the longest x1 3.28 us: shards(): jnp.einsum('hij,ihd->jhd', rounded, upstream, preferred_element_type=jnp....]
    all_to_all x2 -> x0, starting transfers between devices: 8.39 us -> none  [reroute(): lax.all_to_all(buffer, 'seq', split_axis=0, concat_axis=0, tiled=True)]
    gather x4 -> x0, local copies, waits for them, and re-layouts: 7.46 us -> none  [the longest x2 5.39 us: pack(): return padded[slot_table].reshape(seq_count, capacity, values.shape[1])]
    scatter x3 -> x0, local copies, waits for them, and re-layouts: 6.33 us -> none  [the longest x1 3.38 us: shards(): anchor_all = jnp.zeros_like(slide_slot).at[slide_slot].set(every_tile)]
  transfers between devices with their start and end apart: 8 -> 0, of which waited for: 8 -> 0; matrix products, arithmetic and copies ran while one was open for 11% -> 0% of each run, Pallas kernels for 0% -> 0%
where the time goes in v1:
time: 63.8 us; the launch traced here: 62.5 us
  Pallas kernels  48.4 us (76%)
  local copies, waits for them, and re-layouts  13.5 us (21%)
  between operations  0.65 us (1%)
    pallas_call x1, Pallas kernels, fused_shards(): pl.pallas_call(step_kernel, out_shape=(jax.ShapeDtypeStruct((rows, head_c...  48.4 us
    unnamed x21, local copies, waits for them, and re-layouts  10.7 us

profile of v1, /device:TPU:0, one launch (start us, length us, event | category | flops | bytes accessed | tf_op | source)
XLA Modules:
  0.0 62.5 jit_solution(7332665371015771997)
XLA Ops:
  0.6 0.7 %reshape.20.slide_gain_ref = f32[1,768]{1,0:T(1,128)S(1)} reshape(f32[768]{0:T(1024)} %param.19) | data formatting | bytes 6144 | tf_op jit(solution)/shard_map/reshape | solution.py:743
  1.3 0.7 %reshape.21.slot_ref = s32[1,768]{1,0:T(1,128)S(1)} reshape(s32[768]{0:T(1024)} %param.21) | data formatting | bytes 6144 | tf_op jit(solution)/shard_map/reshape | solution.py:745
  2.0 0.7 %reshape.18.layer_scale_ref = f32[1,1536]{1,0:T(1,128)S(1)} reshape(f32[1536]{0:T(1024)} %param.16) | data formatting | bytes 12288 | tf_op jit(solution)/shard_map/reshape | solution.py:740
  2.7 0.7 %reshape.19.tile_gain_ref = f32[1,1536]{1,0:T(1,128)S(1)} reshape(f32[1536]{0:T(1024)} %param.17) | data formatting | bytes 12288 | tf_op jit(solution)/shard_map/reshape | solution.py:741
  3.4 0.0 copy-start
  3.4 1.7 %copy-done = bf16[1536,768]{1,0:T(8,128)(2,1)S(1)} copy-done((bf16[1536,768]{1,0:T(8,128)(2,1)S(1)}, bf16[1536,768]{1,0:T(8,128)(2,1)}, u32[]{:S(2)}) %copy-start) | copy-done | bytes 2359320
  5.1 0.0 copy-start.1
  5.1 1.3 %copy-done.1 = bf16[384,1536]{1,0:T(8,128)(2,1)S(1)} copy-done((bf16[384,1536]{1,0:T(8,128)(2,1)S(1)}, bf16[384,1536]{1,0:T(8,128)(2,1)}, u32[]{:S(2)}) %copy-start.1) | copy-done | bytes 1179672
  6.3 0.0 copy-start.2
  6.4 1.2 %copy-done.2 = bf16[768,3,192]{0,2,1:T(8,128)(2,1)S(1)} copy-done((bf16[768,3,192]{0,2,1:T(8,128)(2,1)S(1)}, bf16[768,3,192]{0,2,1:T(8,128)(2,1)}, u32[]{:S(2)}) %copy-start.2) | copy-done | bytes 884760
  7.5 0.0 copy-start.3
  7.5 0.9 %copy-done.3 = bf16[192,384]{1,0:T(8,128)(2,1)S(1)} copy-done((bf16[192,384]{1,0:T(8,128)(2,1)S(1)}, bf16[192,384]{1,0:T(8,128)(2,1)}, u32[]{:S(2)}) %copy-start.3) | copy-done | bytes 147480
  8.4 0.0 copy-start.4
  8.4 0.9 %copy-done.4 = bf16[192,384]{1,0:T(8,128)(2,1)S(1)} copy-done((bf16[192,384]{1,0:T(8,128)(2,1)S(1)}, bf16[192,384]{1,0:T(8,128)(2,1)}, u32[]{:S(2)}) %copy-start.4) | copy-done | bytes 147480
  9.3 0.0 copy-start.5
  9.3 0.9 %copy-done.5 = bf16[192,192]{1,0:T(8,128)(2,1)S(1)} copy-done((bf16[192,192]{1,0:T(8,128)(2,1)S(1)}, bf16[192,192]{1,0:T(8,128)(2,1)}, u32[]{:S(2)}) %copy-start.5) | copy-done | bytes 73752
  10.2 0.0 copy-start.6
  10.2 0.7 %copy-done.6 = s32[4]{0:T(128)S(1)} copy-done((s32[4]{0:T(128)S(1)}, s32[4]{0:T(128)}, u32[]{:S(2)}) %copy-start.6) | copy-done | bytes 40
  10.9 0.0 copy-start.7
  10.9 0.7 %copy-done.7 = s32[12]{0:T(128)S(1)} copy-done((s32[12]{0:T(128)S(1)}, s32[12]{0:T(128)}, u32[]{:S(2)}) %copy-start.7) | copy-done | bytes 72
  11.5 0.0 copy-start.8
  11.5 0.7 %copy-done.8 = s32[12]{0:T(128)S(1)} copy-done((s32[12]{0:T(128)S(1)}, s32[12]{0:T(128)}, u32[]{:S(2)}) %copy-start.8) | copy-done | bytes 72
  12.2 48.4 %slide_step.1 = (bf16[192,192]{1,0:T(8,128)(2,1)S(1)}, bf16[48,1536]{1,0:T(8,128)(2,1)S(1)}, bf16[192,384]{1,0:T(8,128)(2,1)S(1)}) custom-call(bf16[192,384]{1,0:T(8,128)(2,1)S(1)} %copy-done.3, bf16[192,384]{1,0:T(8,128)(2,1)S(1)} %copy-done.4, bf16[384,1536]{1,0:T(8,128)(2,1)S(1)} %copy-done.1, f32[1,1536]{1,0:T(1,128)S(1)} %reshape.18.layer_scale_ref, ...), custom_call_target="tpu_custom_call" | custom-call | tf_op jit(solution)/shard_map/slide_step/pallas_call | solution.py:676
  60.6 0.6 %copy.19 = bf16[192,192]{1,0:T(8,128)(2,1)} copy(bf16[192,192]{1,0:T(8,128)(2,1)S(1)} %get-tuple-element.6) | data formatting | bytes 147456
  61.2 0.7 %copy.20 = bf16[48,1536]{1,0:T(8,128)(2,1)} copy(bf16[48,1536]{1,0:T(8,128)(2,1)S(1)} %get-tuple-element.7) | data formatting | bytes 294912
  61.9 0.7 %copy.21 = bf16[192,384]{1,0:T(8,128)(2,1)} copy(bf16[192,384]{1,0:T(8,128)(2,1)S(1)} %get-tuple-element.8) | data formatting | bytes 294912
Async XLA Ops:
  3.4 1.7 %copy-start = (bf16[1536,768]{1,0:T(8,128)(2,1)S(1)}, bf16[1536,768]{1,0:T(8,128)(2,1)}, u32[]{:S(2)}) copy-start(bf16[1536,768]{1,0:T(8,128)(2,1)} %slide_proj_hbm.1) | copy-start | bytes 7077892
  5.1 1.3 %copy-start.1 = (bf16[384,1536]{1,0:T(8,128)(2,1)S(1)}, bf16[384,1536]{1,0:T(8,128)(2,1)}, u32[]{:S(2)}) copy-start(bf16[384,1536]{1,0:T(8,128)(2,1)} %out_proj_ref.1) | copy-start | bytes 3538948
  6.3 1.2 %copy-start.2 = (bf16[768,3,192]{0,2,1:T(8,128)(2,1)S(1)}, bf16[768,3,192]{0,2,1:T(8,128)(2,1)}, u32[]{:S(2)}) copy-start(bf16[768,3,192]{0,2,1:T(8,128)(2,1)} %param.20) | copy-start | bytes 2654212
  7.5 0.9 %copy-start.3 = (bf16[192,384]{1,0:T(8,128)(2,1)S(1)}, bf16[192,384]{1,0:T(8,128)(2,1)}, u32[]{:S(2)}) copy-start(bf16[192,384]{1,0:T(8,128)(2,1)} %features_ref.1) | copy-start | bytes 442372
  8.4 0.9 %copy-start.4 = (bf16[192,384]{1,0:T(8,128)(2,1)S(1)}, bf16[192,384]{1,0:T(8,128)(2,1)}, u32[]{:S(2)}) copy-start(bf16[192,384]{1,0:T(8,128)(2,1)} %outputs_ref.1) | copy-start | bytes 442372
  9.3 0.9 %copy-start.5 = (bf16[192,192]{1,0:T(8,128)(2,1)S(1)}, bf16[192,192]{1,0:T(8,128)(2,1)}, u32[]{:S(2)}) copy-start(bf16[192,192]{1,0:T(8,128)(2,1)} %grad_ref.1) | copy-start | bytes 221188
  10.2 0.7 %copy-start.6 = (s32[4]{0:T(128)S(1)}, s32[4]{0:T(128)}, u32[]{:S(2)}) copy-start(s32[4]{0:T(128)} %len_ref.1) | copy-start | bytes 52
  10.9 0.7 %copy-start.7 = (s32[12]{0:T(128)S(1)}, s32[12]{0:T(128)}, u32[]{:S(2)}) copy-start(s32[12]{0:T(128)} %seg_ref.1) | copy-start | bytes 148
  11.5 0.7 %copy-start.8 = (s32[12]{0:T(128)S(1)}, s32[12]{0:T(128)}, u32[]{:S(2)}) copy-start(s32[12]{0:T(128)} %rate_ref.1) | copy-start | bytes 148

commit v2 on v1

--- a/solution.py
+++ b/solution.py
@@ -265,6 +265,7 @@
 HIDDEN = -1e30
 GROUP_SEQ = 1 << SPAN_LOG
 QUAD = 4
+VMEM_LIMIT = 65472 * 1024
 
 
 def rows_dot(left, right):
@@ -280,24 +281,31 @@
 
 
 def step_kernel(
+    features_hbm,
+    outputs_hbm,
+    out_proj_hbm,
+    layer_scale_hbm,
+    tile_gain_hbm,
+    slide_proj_hbm,
+    slide_gain_hbm,
+    weight_hbm,
+    slot_hbm,
+    len_ref,
+    seg_ref,
+    rate_ref,
+    grad_hbm,
+    heads_out,
+    tile_out,
+    head_out,
     features_ref,
     outputs_ref,
     out_proj_ref,
     layer_scale_ref,
     tile_gain_ref,
-    slide_proj_hbm,
+    slide_proj_ref,
     slide_gain_ref,
-    weight_hbm,
+    weight_ref,
     slot_ref,
-    len_ref,
-    seg_ref,
-    rate_ref,
-    grad_ref,
-    heads_out,
-    tile_out,
-    head_out,
-    slide_proj_ref,
-    weight_ref,
     upstream_all,
     term_ref,
     first_out,
@@ -345,7 +353,7 @@
     rows, width_part = features_ref.shape
     total = GROUP_SEQ * rows
     share = rows // QUAD
-    head_cols = grad_ref.shape[1]
+    head_cols = grad_hbm.shape[1]
     local_heads = head_cols // HEAD_DIM
     seq = lax.axis_index("seq")
     mp = lax.axis_index("mp")
@@ -363,11 +371,6 @@
             device_id_type=MESH,
         )
 
-    slide_load = pltpu.make_async_copy(slide_proj_hbm, slide_proj_ref, load_sem.at[0])
-    weight_load = pltpu.make_async_copy(weight_hbm, weight_ref, load_sem.at[1])
-    slide_load.start()
-    weight_load.start()
-
     barrier = pltpu.get_barrier_semaphore()
     for offset in range(1, GROUP_SEQ):
         pl.semaphore_signal(
@@ -378,7 +381,29 @@
             barrier, inc=1, device_id={"mp": (mp + offset) % QUAD}, device_id_type=MESH
         )
 
-    term_ref[...] = layer_scale_ref[...] * plain_dot(outputs_ref[...], out_proj_ref[...])
+    loads = [
+        pltpu.make_async_copy(source, target, load_sem.at[index])
+        for index, (source, target) in enumerate(
+            (
+                (outputs_hbm, outputs_ref),
+                (out_proj_hbm, out_proj_ref),
+                (layer_scale_hbm, layer_scale_ref),
+                (features_hbm, features_ref),
+                (slot_hbm, slot_ref),
+                (tile_gain_hbm, tile_gain_ref),
+                (slide_gain_hbm, slide_gain_ref),
+                (grad_hbm, upstream_all.at[seq]),
+                (slide_proj_hbm, slide_proj_ref),
+                (weight_hbm, weight_ref),
+            )
+        )
+    ]
+    for load in loads:
+        load.start()
+    for load in loads[:4]:
+        load.wait()
+    layer_scale = layer_scale_ref[...].reshape(1, layer_scale_ref.shape[0])
+    term_ref[...] = layer_scale * plain_dot(outputs_ref[...], out_proj_ref[...])
     own_cols = pl.ds(pl.multiple_of(mp * width_part, 128), width_part)
     term_ref[:, own_cols] += features_ref[...].astype(F32)
 
@@ -403,20 +428,22 @@
         out_ref[...] = (source[share_of(across), :] + in_buf[1].astype(F32)).astype(BF16)
         copy = remote(out_ref, in_ref, send.at[2], recv.at[2], {"mp": across})
         copy.start()
+        return copies + [copy]
+
+    def scatter_third(source, copies, in_buf, in_ref):
         copies[1].wait_recv()
         partial = source[share_of(mp), :] + in_buf[0].astype(F32)
-        copy.wait_recv()
-        for each in copies + [copy]:
+        copies[2].wait_recv()
+        for each in copies:
             each.wait_send()
         return partial + in_ref[...].astype(F32)
 
     first = scatter_first(term_ref, first_out, first_in, scatter_send, scatter_recv)
 
-    upstream_all[seq] = grad_ref[...]
     up_copies = []
     for offset in range(1, GROUP_SEQ):
         copy = remote(
-            grad_ref,
+            grad_hbm,
             upstream_all.at[seq],
             up_send.at[offset - 1],
             up_recv.at[offset - 1],
@@ -425,7 +452,14 @@
         copy.start()
         up_copies.append(copy)
 
-    slots = slot_ref[...]
+    second = scatter_second(
+        term_ref, first, first_in, second_out, second_in, scatter_send, scatter_recv
+    )
+    for load in loads[4:8]:
+        load.wait()
+    slots = slot_ref[...].reshape(1, total)
+    tile_gain = tile_gain_ref[...].reshape(1, tile_gain_ref.shape[0])
+    slide_gain = slide_gain_ref[...].reshape(1, slide_gain_ref.shape[0])
     base = seq * rows
     bounds = []
     reached = 0
@@ -467,15 +501,13 @@
         jnp.broadcast_to(slots, (total, total)) == lax.broadcasted_iota(jnp.int32, (total, total), 0)
     ).astype(BF16)
 
-    summed = scatter_second(
-        term_ref, first, first_in, second_out, second_in, scatter_send, scatter_recv
-    )
+    summed = scatter_third(term_ref, second, first_in, second_in)
     tile_normed, tile_inverse = norm_parts(summed)
-    lifted = (tile_normed * tile_gain_ref[...]).astype(BF16)
-    slide_load.wait()
+    lifted = (tile_normed * tile_gain).astype(BF16)
+    loads[8].wait()
     embedded = plain_dot(lifted, slide_proj_ref[...])
     slide_normed, slide_inverse = norm_parts(embedded)
-    entering_all[seq, mp] = (slide_normed * slide_gain_ref[...]).astype(BF16)
+    entering_all[seq, mp] = (slide_normed * slide_gain).astype(BF16)
 
     pending = []
 
@@ -528,7 +560,7 @@
                 {"mp": sibling},
             )
         )
-    weight_load.wait()
+    loads[9].wait()
     for copy in core_copies:
         copy.wait_recv()
     entering = entering_all[...].reshape(total, entering_all.shape[3])
@@ -611,15 +643,16 @@
         + plain_dot(value_sum.astype(BF16), weight_ref[2])
     )
     back_first = scatter_first(back_ref, back_first_out, back_first_in, back_send, back_recv)
-    entering_grad = scatter_second(
+    back_second = scatter_second(
         back_ref, back_first, back_first_in, back_second_out, back_second_in, back_send, back_recv
     )
+    entering_grad = scatter_third(back_ref, back_second, back_first_in, back_second_in)
     embedded_grad = norm_back(
-        entering_grad * slide_gain_ref[...], slide_normed, slide_inverse
+        entering_grad * slide_gain, slide_normed, slide_inverse
     ).astype(BF16)
     lifted_grad = rows_dot(embedded_grad, slide_proj_ref[...])
-    summed_grad = norm_back(lifted_grad * tile_gain_ref[...], tile_normed, tile_inverse)
-    mixed_all[mp] = (layer_scale_ref[...] * summed_grad).astype(BF16)
+    summed_grad = norm_back(lifted_grad * tile_gain, tile_normed, tile_inverse)
+    mixed_all[mp] = (layer_scale * summed_grad).astype(BF16)
 
     def mixed_move(place, index, where):
         copy = remote(
@@ -671,7 +704,7 @@
     total = GROUP_SEQ * rows
     vmem = pl.BlockSpec(memory_space=pltpu.VMEM)
     smem = pl.BlockSpec(memory_space=pltpu.SMEM)
-    hbm = pl.BlockSpec(memory_space=pl.ANY)
+    hbm = pl.BlockSpec(memory_space=pltpu.HBM)
     dma = pltpu.SemaphoreType.DMA
     return pl.pallas_call(
         step_kernel,
@@ -680,11 +713,18 @@
             jax.ShapeDtypeStruct((share, width), BF16),
             jax.ShapeDtypeStruct((rows, width_part), BF16),
         ),
-        in_specs=[vmem, vmem, vmem, vmem, vmem, hbm, vmem, hbm, vmem, smem, smem, smem, vmem],
+        in_specs=[hbm] * 9 + [smem] * 3 + [hbm],
         out_specs=(vmem, vmem, vmem),
         scratch_shapes=[
+            pltpu.VMEM((rows, width_part), BF16),
+            pltpu.VMEM((rows, width_part), BF16),
+            pltpu.VMEM((width_part, width), BF16),
+            pltpu.VMEM((width,), F32),
+            pltpu.VMEM((width,), F32),
             pltpu.VMEM((width, slide_width), BF16),
+            pltpu.VMEM((slide_width,), F32),
             pltpu.VMEM((3, head_cols, slide_width), BF16),
+            pltpu.VMEM((total,), jnp.int32),
             pltpu.VMEM((GROUP_SEQ, rows, head_cols), BF16),
             pltpu.VMEM((rows, width), F32),
             pltpu.VMEM((2, share, width), BF16),
@@ -709,7 +749,7 @@
             pltpu.VMEM((share, slide_width), BF16),
             pltpu.VMEM((share, slide_width), BF16),
             pltpu.VMEM((QUAD, share, width), BF16),
-            dma((2,)),
+            dma((10,)),
             dma((3,)),
             dma((3,)),
             dma((3,)),
@@ -730,19 +770,19 @@
             dma((3,)),
         ],
         compiler_params=pltpu.CompilerParams(
-            collective_id=0, has_side_effects=True, vmem_limit_bytes=48 * 1024 * 1024
+            collective_id=0, has_side_effects=True, vmem_limit_bytes=VMEM_LIMIT
         ),
         name="slide_step",
     )(
         tile_features,
         head_outputs,
         out_proj,
-        layer_scale.reshape(1, width),
-        tile_gain.reshape(1, width),
+        layer_scale,
+        tile_gain,
         slide_proj,
-        slide_gain.reshape(1, slide_width),
+        slide_gain,
         jnp.transpose(qkv_weight, (1, 2, 0)),
-        slide_slot.reshape(1, total),
+        slide_slot,
         slide_len,
         seg_log,
         rate_log,

time: 63.8 us -> 56.3 us (0.88)
  the two profiles are of different devices: /device:TPU:0 before, /device:TPU:9 now
where the time goes in v2:
time: 56.3 us; the launch traced here: 56.1 us
  Pallas kernels  50.8 us (90%)
  local copies, waits for them, and re-layouts  4.7 us (8%)
  between operations  0.64 us (1%)
    pallas_call x1, Pallas kernels, fused_shards(): pl.pallas_call(step_kernel, out_shape=(jax.ShapeDtypeStruct((rows, head_c...  50.8 us
    unnamed x3, local copies, waits for them, and re-layouts  4.7 us

profile of v2, /device:TPU:9, one launch (start us, length us, event | category | flops | bytes accessed | tf_op | source)
XLA Modules:
  0.0 56.1 jit_solution(17789009781433543549)
XLA Ops:
  0.6 50.8 %slide_step.1 = (bf16[192,192]{1,0:T(8,128)(2,1)}, bf16[48,1536]{1,0:T(8,128)(2,1)}, bf16[192,384]{1,0:T(8,128)(2,1)}) custom-call(bf16[192,384]{1,0:T(8,128)(2,1)} %features_hbm.1, bf16[192,384]{1,0:T(8,128)(2,1)} %outputs_hbm.1, bf16[384,1536]{1,0:T(8,128)(2,1)} %out_proj_hbm.1, f32[1536]{0:T(1024)} %layer_scale_hbm.1, f32[1536]{0:T(1024)} %tile_gain_hbm.1, ...), custom_call_target="tpu_custom_call" | custom-call | tf_op jit(solution)/shard_map/slide_step/pallas_call | solution.py:709
  51.4 1.5 %copy.19 = bf16[192,192]{1,0:T(8,128)(2,1)} copy(bf16[192,192]{1,0:T(8,128)(2,1)} %get-tuple-element.6) | data formatting | bytes 147456
  53.0 1.6 %copy.20 = bf16[48,1536]{1,0:T(8,128)(2,1)} copy(bf16[48,1536]{1,0:T(8,128)(2,1)} %get-tuple-element.7) | data formatting | bytes 294912
  54.5 1.6 %copy.21 = bf16[192,384]{1,0:T(8,128)(2,1)} copy(bf16[192,384]{1,0:T(8,128)(2,1)} %get-tuple-element.8) | data formatting | bytes 294912

commit v3 on v2

--- a/solution.py
+++ b/solution.py
@@ -322,6 +322,7 @@
     score_buf,
     grad_buf,
     stats_pad,
+    stats_line,
     stats_all,
     heads_all,
     back_ref,
@@ -537,6 +538,17 @@
     x_copies = [forward(seq, mp, x_send.at[0], x_recv.at[0], {"mp": across})]
     core_copies = [forward(seq, mp, core_send.at[0], core_recv.at[0], {"mp": sibling})]
 
+    def project(offset):
+        core_copies[offset].wait_recv()
+        core_copies[GROUP_SEQ + offset].wait_recv()
+        origin = (seq + GROUP_SEQ - offset) % GROUP_SEQ
+        entering = entering_all[origin].reshape(rows, entering_all.shape[3])
+        block = pl.ds(pl.multiple_of(origin * rows, 64), rows)
+        query = rows_dot(entering, weight_ref[0]).astype(BF16)
+        query_ref[block, :] = (query.astype(F32) * SCALE).astype(BF16)
+        key_ref[block, :] = rows_dot(entering, weight_ref[1]).astype(BF16)
+        value_ref[block, :] = rows_dot(entering, weight_ref[2]).astype(BF16)
+
     for copy in up_copies:
         copy.wait()
     upstream_ref[...] = cols_dot(arrange, upstream_all[...].reshape(total, head_cols)).astype(BF16)
@@ -548,6 +560,7 @@
         core_copies.append(
             forward(origin, mp, core_send.at[offset], core_recv.at[offset], {"mp": sibling})
         )
+    loads[9].wait()
     for offset in range(GROUP_SEQ):
         origin = (seq + GROUP_SEQ - offset) % GROUP_SEQ
         x_copies[offset].wait_recv()
@@ -560,15 +573,9 @@
                 {"mp": sibling},
             )
         )
-    loads[9].wait()
-    for copy in core_copies:
-        copy.wait_recv()
-    entering = entering_all[...].reshape(total, entering_all.shape[3])
-    query_ref[...] = (rows_dot(entering, weight_ref[0]).astype(BF16).astype(F32) * SCALE).astype(
-        BF16
-    )
-    key_ref[...] = rows_dot(entering, weight_ref[1]).astype(BF16)
-    value_ref[...] = rows_dot(entering, weight_ref[2]).astype(BF16)
+        if offset > 0:
+            project(offset - 1)
+    project(GROUP_SEQ - 1)
     for copy in pending:
         copy.wait_send()
 
@@ -596,7 +603,7 @@
         score_grad = (probability * (prob_grad - delta)).astype(BF16)
         heads_sum = heads_sum + cols_dot(probability.astype(BF16), head_only(values, head))
         query_sum = query_sum + cols_dot(score_grad, head_only(keys, head))
-    stats_all[seq] = pltpu.roll(stats_pad[...], base, 1)
+    stats_all[seq] = stats_pad[...]
     heads_all[seq] = heads_sum.astype(BF16)
     stats_copies = []
     heads_copies = []
@@ -629,7 +636,9 @@
         grad_buf[head] = rows_dot(own_values, head_only(upstream, head))
     for copy in stats_copies:
         copy.wait()
-    stats = stats_all[0] + stats_all[1] + stats_all[2] + stats_all[3]
+    for origin in range(GROUP_SEQ):
+        stats_line[:, origin * rows : (origin + 1) * rows] = stats_all[origin, :, :rows]
+    stats = stats_line[...]
     key_sum = jnp.zeros((rows, head_cols), F32)
     value_sum = jnp.zeros((rows, head_cols), F32)
     for head in range(local_heads):
@@ -678,6 +687,18 @@
     head_out[...] = rows_dot(
         mixed_all[...].reshape(rows, mixed_all.shape[2]), out_proj_ref[...]
     ).astype(BF16)
+
+
+def finish_kernel(heads_in, tile_in, head_in, heads_out, tile_out, head_out, sems):
+    pairs = ((heads_in, heads_out), (tile_in, tile_out), (head_in, head_out))
+    copies = [
+        pltpu.make_async_copy(source, target, sems.at[index])
+        for index, (source, target) in enumerate(pairs)
+    ]
+    for copy in copies:
+        copy.start()
+    for copy in copies:
+        copy.wait()
 
 
 def fused_shards(
@@ -702,17 +723,19 @@
     local_heads = head_cols // HEAD_DIM
     share = rows // QUAD
     total = GROUP_SEQ * rows
+    stats_lanes = -(-rows // 128) * 128
     vmem = pl.BlockSpec(memory_space=pltpu.VMEM)
     smem = pl.BlockSpec(memory_space=pltpu.SMEM)
     hbm = pl.BlockSpec(memory_space=pltpu.HBM)
     dma = pltpu.SemaphoreType.DMA
-    return pl.pallas_call(
+    results = (
+        jax.ShapeDtypeStruct((rows, head_cols), BF16),
+        jax.ShapeDtypeStruct((share, width), BF16),
+        jax.ShapeDtypeStruct((rows, width_part), BF16),
+    )
+    computed = pl.pallas_call(
         step_kernel,
-        out_shape=(
-            jax.ShapeDtypeStruct((rows, head_cols), BF16),
-            jax.ShapeDtypeStruct((share, width), BF16),
-            jax.ShapeDtypeStruct((rows, width_part), BF16),
-        ),
+        out_shape=results,
         in_specs=[hbm] * 9 + [smem] * 3 + [hbm],
         out_specs=(vmem, vmem, vmem),
         scratch_shapes=[
@@ -740,8 +763,9 @@
             pltpu.VMEM((local_heads, rows, total), F32),
             pltpu.VMEM((local_heads, rows, total), F32),
             pltpu.VMEM((local_heads, rows, total), F32),
+            pltpu.VMEM((8, stats_lanes), F32),
             pltpu.VMEM((8, total), F32),
-            pltpu.VMEM((GROUP_SEQ, 8, total), F32),
+            pltpu.VMEM((GROUP_SEQ, 8, stats_lanes), F32),
             pltpu.VMEM((GROUP_SEQ, rows, head_cols), BF16),
             pltpu.VMEM((rows, slide_width), F32),
             pltpu.VMEM((2, share, slide_width), BF16),
@@ -788,6 +812,15 @@
         rate_log,
         out_grad,
     )
+    return pl.pallas_call(
+        finish_kernel,
+        out_shape=results,
+        in_specs=[hbm] * 3,
+        out_specs=(hbm,) * 3,
+        scratch_shapes=[dma((3,))],
+        compiler_params=pltpu.CompilerParams(vmem_limit_bytes=VMEM_LIMIT),
+        name="finish",
+    )(*computed)
 
 
 def solution(mesh):

time: 56.3 us -> 62.8 us (1.12)
  the two profiles are of different devices: /device:TPU:9 before, /device:TPU:0 now
where the time goes in v3:
time: 62.8 us; the launch traced here: 62.6 us
  Pallas kernels  62 us (99%)
  between operations  0.64 us (1%)
    pallas_call x1, Pallas kernels, fused_shards(): pl.pallas_call(step_kernel, out_shape=results, in_specs=[hbm] * 9 + [smem...  48.9 us
    pallas_call x1, Pallas kernels, fused_shards(): pl.pallas_call(finish_kernel, out_shape=results, in_specs=[hbm] * 3, out_...  13 us

profile of v3, /device:TPU:0, one launch (start us, length us, event | category | flops | bytes accessed | tf_op | source)
XLA Modules:
  0.0 62.6 jit_solution(13148872989449414039)
XLA Ops:
  0.6 48.9 %slide_step.1 = (bf16[192,192]{1,0:T(8,128)(2,1)}, bf16[48,1536]{1,0:T(8,128)(2,1)}, bf16[192,384]{1,0:T(8,128)(2,1)}) custom-call(bf16[192,384]{1,0:T(8,128)(2,1)} %features_hbm.1, bf16[192,384]{1,0:T(8,128)(2,1)} %outputs_hbm.1, bf16[384,1536]{1,0:T(8,128)(2,1)} %out_proj_hbm.1, f32[1536]{0:T(1024)} %layer_scale_hbm.1, f32[1536]{0:T(1024)} %tile_gain_hbm.1, ...), custom_call_target="tpu_custom_call" | custom-call | tf_op jit(solution)/shard_map/slide_step/pallas_call | solution.py:736
  49.6 13.0 %finish.1 = (bf16[192,192]{1,0:T(8,128)(2,1)}, bf16[48,1536]{1,0:T(8,128)(2,1)}, bf16[192,384]{1,0:T(8,128)(2,1)}) custom-call(bf16[192,192]{1,0:T(8,128)(2,1)} %get-tuple-element.6.heads_in, bf16[48,1536]{1,0:T(8,128)(2,1)} %get-tuple-element.7.tile_in, bf16[192,384]{1,0:T(8,128)(2,1)} %get-tuple-element.8.head_in), custom_call_target="tpu_custom_call" | custom-call | tf_op jit(solution)/shard_map/finish/pallas_call | solution.py:815

commit v4 on v3

--- a/solution.py
+++ b/solution.py
@@ -331,6 +331,8 @@
     back_second_out,
     back_second_in,
     mixed_all,
+    summed_out,
+    summed_in,
     load_sem,
     up_send,
     up_recv,
@@ -503,12 +505,16 @@
     ).astype(BF16)
 
     summed = scatter_third(term_ref, second, first_in, second_in)
-    tile_normed, tile_inverse = norm_parts(summed)
-    lifted = (tile_normed * tile_gain).astype(BF16)
     loads[8].wait()
-    embedded = plain_dot(lifted, slide_proj_ref[...])
-    slide_normed, slide_inverse = norm_parts(embedded)
-    entering_all[seq, mp] = (slide_normed * slide_gain).astype(BF16)
+
+    def norms_of(block):
+        tile_normed, tile_inverse = norm_parts(block)
+        lifted = (tile_normed * tile_gain).astype(BF16)
+        slide_normed, slide_inverse = norm_parts(plain_dot(lifted, slide_proj_ref[...]))
+        return tile_normed, tile_inverse, slide_normed, slide_inverse
+
+    own_norms = norms_of(summed)
+    entering_all[seq, mp] = (own_norms[2] * slide_gain).astype(BF16)
 
     pending = []
 
@@ -560,6 +566,11 @@
         core_copies.append(
             forward(origin, mp, core_send.at[offset], core_recv.at[offset], {"mp": sibling})
         )
+    summed_out[...] = summed
+    summed_copy = remote(
+        summed_out, summed_in, mixed_send.at[0], mixed_recv.at[0], {"mp": across}
+    )
+    summed_copy.start()
     loads[9].wait()
     for offset in range(GROUP_SEQ):
         origin = (seq + GROUP_SEQ - offset) % GROUP_SEQ
@@ -634,6 +645,10 @@
     for head in range(local_heads):
         score_buf[head] = rows_dot(own_keys, head_only(queries, head)) + bias_col[head]
         grad_buf[head] = rows_dot(own_values, head_only(upstream, head))
+    summed_copy.wait()
+    tile_normed, tile_inverse, slide_normed, slide_inverse = (
+        jnp.concatenate(pair, axis=0) for pair in zip(own_norms, norms_of(summed_in[...]))
+    )
     for copy in stats_copies:
         copy.wait()
     for origin in range(GROUP_SEQ):
@@ -652,16 +667,34 @@
         + plain_dot(value_sum.astype(BF16), weight_ref[2])
     )
     back_first = scatter_first(back_ref, back_first_out, back_first_in, back_send, back_recv)
-    back_second = scatter_second(
-        back_ref, back_first, back_first_in, back_second_out, back_second_in, back_send, back_recv
-    )
-    entering_grad = scatter_third(back_ref, back_second, back_first_in, back_second_in)
+    back_first[0].wait_recv()
+    partial_across = back_ref[share_of(across), :] + back_first_in[1].astype(F32)
+    back_first[1].wait_recv()
+    partial_own = back_ref[share_of(mp), :] + back_first_in[0].astype(F32)
+    back_second_out[0] = partial_own.astype(BF16)
+    back_second_out[1] = partial_across.astype(BF16)
+    back_copy = remote(
+        back_second_out, back_second_in, back_send.at[2], back_recv.at[2], {"mp": across}
+    )
+    back_copy.start()
+    for copy in back_first:
+        copy.wait_send()
+    back_copy.wait()
+    entering_grad = jnp.concatenate(
+        [
+            partial_own + back_second_in[1].astype(F32),
+            partial_across + back_second_in[0].astype(F32),
+        ],
+        axis=0,
+    )
     embedded_grad = norm_back(
         entering_grad * slide_gain, slide_normed, slide_inverse
     ).astype(BF16)
     lifted_grad = rows_dot(embedded_grad, slide_proj_ref[...])
     summed_grad = norm_back(lifted_grad * tile_gain, tile_normed, tile_inverse)
-    mixed_all[mp] = (layer_scale * summed_grad).astype(BF16)
+    mixed = (layer_scale * summed_grad).astype(BF16)
+    mixed_all[mp] = mixed[:share]
+    mixed_all[across] = mixed[share:]
 
     def mixed_move(place, index, where):
         copy = remote(
@@ -674,14 +707,12 @@
         copy.start()
         return copy
 
-    mixed_x = mixed_move(mp, 0, across)
     mixed_core = mixed_move(mp, 1, sibling)
-    tile_out[...] = summed_grad.astype(BF16)
+    mixed_corner = mixed_move(across, 2, sibling)
+    tile_out[...] = summed_grad[:share].astype(BF16)
     for copy in heads_copies:
         copy.wait()
     heads_out[...] = plain_dot(pick_heads, heads_all[...].reshape(total, head_cols)).astype(BF16)
-    mixed_x.wait()
-    mixed_corner = mixed_move(across, 2, sibling)
     mixed_core.wait()
     mixed_corner.wait()
     head_out[...] = rows_dot(
@@ -689,16 +720,26 @@
     ).astype(BF16)
 
 
-def finish_kernel(heads_in, tile_in, head_in, heads_out, tile_out, head_out, sems):
-    pairs = ((heads_in, heads_out), (tile_in, tile_out), (head_in, head_out))
-    copies = [
-        pltpu.make_async_copy(source, target, sems.at[index])
-        for index, (source, target) in enumerate(pairs)
-    ]
-    for copy in copies:
-        copy.start()
-    for copy in copies:
-        copy.wait()
+def finish_kernel(
+    heads_in, tile_in, head_in, heads_out, tile_out, head_out, heads_mid, tile_mid, head_mid, sems
+):
+    triples = (
+        (heads_in, heads_mid, heads_out),
+        (tile_in, tile_mid, tile_out),
+        (head_in, head_mid, head_out),
+    )
+    loads = []
+    stores = []
+    for index, (source, middle, target) in enumerate(triples):
+        loads.append(pltpu.make_async_copy(source, middle, sems.at[0, index]))
+        stores.append(pltpu.make_async_copy(middle, target, sems.at[1, index]))
+    for load in loads:
+        load.start()
+    for load, store in zip(loads, stores):
+        load.wait()
+        store.start()
+    for store in stores:
+        store.wait()
 
 
 def fused_shards(
@@ -770,9 +811,11 @@
             pltpu.VMEM((rows, slide_width), F32),
             pltpu.VMEM((2, share, slide_width), BF16),
             pltpu.VMEM((2, share, slide_width), BF16),
-            pltpu.VMEM((share, slide_width), BF16),
-            pltpu.VMEM((share, slide_width), BF16),
+            pltpu.VMEM((2, share, slide_width), BF16),
+            pltpu.VMEM((2, share, slide_width), BF16),
             pltpu.VMEM((QUAD, share, width), BF16),
+            pltpu.VMEM((share, width), F32),
+            pltpu.VMEM((share, width), F32),
             dma((10,)),
             dma((3,)),
             dma((3,)),
@@ -817,7 +860,7 @@
         out_shape=results,
         in_specs=[hbm] * 3,
         out_specs=(hbm,) * 3,
-        scratch_shapes=[dma((3,))],
+        scratch_shapes=[pltpu.VMEM(each.shape, each.dtype) for each in results] + [dma((2, 3))],
         compiler_params=pltpu.CompilerParams(vmem_limit_bytes=VMEM_LIMIT),
         name="finish",
     )(*computed)

time: 62.8 us -> 49.6 us (0.79)
  Pallas kernels: 62 us -> 48.8 us
    pallas_call x1, Pallas kernels: 13 us -> 1.74 us  [fused_shards(): pl.pallas_call(finish_kernel, out_shape=results, in_specs=[hbm] * 3, out_...]
    pallas_call x1, Pallas kernels: 48.9 us -> 47.1 us  [fused_shards(): pl.pallas_call(step_kernel, out_shape=results, in_specs=[hbm] * 9 + [smem...]
where the time goes in v4:
time: 49.6 us; the launch traced here: 49.5 us
  Pallas kernels  48.8 us (98%)
  between operations  0.64 us (1%)
    pallas_call x1, Pallas kernels, fused_shards(): pl.pallas_call(step_kernel, out_shape=results, in_specs=[hbm] * 9 + [smem...  47.1 us
    pallas_call x1, Pallas kernels, fused_shards(): pl.pallas_call(finish_kernel, out_shape=results, in_specs=[hbm] * 3, out_...  1.74 us

profile of v4, /device:TPU:0, one launch (start us, length us, event | category | flops | bytes accessed | tf_op | source)
XLA Modules:
  0.0 49.5 jit_solution(14402842896323224835)
XLA Ops:
  0.6 47.1 %slide_step.1 = (bf16[192,192]{1,0:T(8,128)(2,1)}, bf16[48,1536]{1,0:T(8,128)(2,1)}, bf16[192,384]{1,0:T(8,128)(2,1)}) custom-call(bf16[192,384]{1,0:T(8,128)(2,1)} %features_hbm.1, bf16[192,384]{1,0:T(8,128)(2,1)} %outputs_hbm.1, bf16[384,1536]{1,0:T(8,128)(2,1)} %out_proj_hbm.1, f32[1536]{0:T(1024)} %layer_scale_hbm.1, f32[1536]{0:T(1024)} %tile_gain_hbm.1, ...), custom_call_target="tpu_custom_call" | custom-call | tf_op jit(solution)/shard_map/slide_step/pallas_call | solution.py:777
  47.7 1.7 %finish.1 = (bf16[192,192]{1,0:T(8,128)(2,1)}, bf16[48,1536]{1,0:T(8,128)(2,1)}, bf16[192,384]{1,0:T(8,128)(2,1)}) custom-call(bf16[192,192]{1,0:T(8,128)(2,1)} %get-tuple-element.6.heads_in, bf16[48,1536]{1,0:T(8,128)(2,1)} %get-tuple-element.7.tile_in, bf16[192,384]{1,0:T(8,128)(2,1)} %get-tuple-element.8.head_in), custom_call_target="tpu_custom_call" | custom-call | tf_op jit(solution)/shard_map/finish/pallas_call | solution.py:858

commit v5 on v4

--- a/solution.py
+++ b/solution.py
@@ -319,6 +319,8 @@
     upstream_ref,
     bias_row,
     bias_col,
+    rounded_buf,
+    score_grad_buf,
     score_buf,
     grad_buf,
     stats_pad,
@@ -611,11 +613,9 @@
         delta = jnp.sum(probability * prob_grad, axis=0, keepdims=True)
         stats_pad[2 * head : 2 * head + 1, :rows] = row_max + jnp.log(row_sum)
         stats_pad[2 * head + 1 : 2 * head + 2, :rows] = delta
-        score_grad = (probability * (prob_grad - delta)).astype(BF16)
-        heads_sum = heads_sum + cols_dot(probability.astype(BF16), head_only(values, head))
-        query_sum = query_sum + cols_dot(score_grad, head_only(keys, head))
+        rounded_buf[head] = probability.astype(BF16)
+        score_grad_buf[head] = (probability * (prob_grad - delta)).astype(BF16)
     stats_all[seq] = stats_pad[...]
-    heads_all[seq] = heads_sum.astype(BF16)
     stats_copies = []
     heads_copies = []
     for offset in range(1, GROUP_SEQ):
@@ -628,6 +628,10 @@
         )
         copy.start()
         stats_copies.append(copy)
+    for head in range(local_heads):
+        heads_sum = heads_sum + cols_dot(rounded_buf[head], head_only(values, head))
+        query_sum = query_sum + cols_dot(score_grad_buf[head], head_only(keys, head))
+    heads_all[seq] = heads_sum.astype(BF16)
     for offset in range(1, GROUP_SEQ):
         copy = remote(
             heads_all.at[seq],
@@ -649,6 +653,7 @@
     tile_normed, tile_inverse, slide_normed, slide_inverse = (
         jnp.concatenate(pair, axis=0) for pair in zip(own_norms, norms_of(summed_in[...]))
     )
+    back_ref[...] = plain_dot((query_sum * SCALE).astype(BF16), weight_ref[0])
     for copy in stats_copies:
         copy.wait()
     for origin in range(GROUP_SEQ):
@@ -661,9 +666,8 @@
         score_grad = probability * (grad_buf[head] - stats[2 * head + 1 : 2 * head + 2])
         value_sum = value_sum + plain_dot(probability.astype(BF16), head_only(upstream, head))
         key_sum = key_sum + plain_dot(score_grad.astype(BF16), head_only(queries, head))
-    back_ref[...] = (
-        plain_dot((query_sum * SCALE).astype(BF16), weight_ref[0])
-        + plain_dot(key_sum.astype(BF16), weight_ref[1])
+    back_ref[...] += (
+        plain_dot(key_sum.astype(BF16), weight_ref[1])
         + plain_dot(value_sum.astype(BF16), weight_ref[2])
     )
     back_first = scatter_first(back_ref, back_first_out, back_first_in, back_send, back_recv)
@@ -802,6 +806,8 @@
             pltpu.VMEM((total, head_cols), BF16),
             pltpu.VMEM((local_heads, total, rows), F32),
             pltpu.VMEM((local_heads, rows, total), F32),
+            pltpu.VMEM((local_heads, total, rows), BF16),
+            pltpu.VMEM((local_heads, total, rows), BF16),
             pltpu.VMEM((local_heads, rows, total), F32),
             pltpu.VMEM((local_heads, rows, total), F32),
             pltpu.VMEM((8, stats_lanes), F32),

time: 49.6 us -> 48.9 us (0.986)
  Pallas kernels: 48.8 us -> 48.1 us
    pallas_call x1, Pallas kernels: 47.1 us -> 46.4 us  [fused_shards(): pl.pallas_call(step_kernel, out_shape=results, in_specs=[hbm] * 9 + [smem...]
where the time goes in v5:
time: 48.9 us; the launch traced here: 48.7 us
  Pallas kernels  48.1 us (98%)
  between operations  0.64 us (1%)
    pallas_call x1, Pallas kernels, fused_shards(): pl.pallas_call(step_kernel, out_shape=results, in_specs=[hbm] * 9 + [smem...  46.4 us
    pallas_call x1, Pallas kernels, fused_shards(): pl.pallas_call(finish_kernel, out_shape=results, in_specs=[hbm] * 3, out_...  1.74 us

profile of v5, /device:TPU:0, one launch (start us, length us, event | category | flops | bytes accessed | tf_op | source)
XLA Modules:
  0.0 48.7 jit_solution(13294029836505443391)
XLA Ops:
  0.6 46.4 %slide_step.1 = (bf16[192,192]{1,0:T(8,128)(2,1)}, bf16[48,1536]{1,0:T(8,128)(2,1)}, bf16[192,384]{1,0:T(8,128)(2,1)}) custom-call(bf16[192,384]{1,0:T(8,128)(2,1)} %features_hbm.1, bf16[192,384]{1,0:T(8,128)(2,1)} %outputs_hbm.1, bf16[384,1536]{1,0:T(8,128)(2,1)} %out_proj_hbm.1, f32[1536]{0:T(1024)} %layer_scale_hbm.1, f32[1536]{0:T(1024)} %tile_gain_hbm.1, ...), custom_call_target="tpu_custom_call" | custom-call | tf_op jit(solution)/shard_map/slide_step/pallas_call | solution.py:781
  47.0 1.7 %finish.1 = (bf16[192,192]{1,0:T(8,128)(2,1)}, bf16[48,1536]{1,0:T(8,128)(2,1)}, bf16[192,384]{1,0:T(8,128)(2,1)}) custom-call(bf16[192,192]{1,0:T(8,128)(2,1)} %get-tuple-element.6.heads_in, bf16[48,1536]{1,0:T(8,128)(2,1)} %get-tuple-element.7.tile_in, bf16[192,384]{1,0:T(8,128)(2,1)} %get-tuple-element.8.head_in), custom_call_target="tpu_custom_call" | custom-call | tf_op jit(solution)/shard_map/finish/pallas_call | solution.py:864

commit v6 on v5

--- a/solution.py
+++ b/solution.py
@@ -717,11 +717,17 @@
     for copy in heads_copies:
         copy.wait()
     heads_out[...] = plain_dot(pick_heads, heads_all[...].reshape(total, head_cols)).astype(BF16)
+
+    def head_rows(first_place, second_place):
+        block = jnp.concatenate([mixed_all[first_place], mixed_all[second_place]], axis=0)
+        product = rows_dot(block, out_proj_ref[...]).astype(BF16)
+        head_out[share_of(first_place), :] = product[:share]
+        head_out[share_of(second_place), :] = product[share:]
+
+    head_rows(mp, across)
     mixed_core.wait()
     mixed_corner.wait()
-    head_out[...] = rows_dot(
-        mixed_all[...].reshape(rows, mixed_all.shape[2]), out_proj_ref[...]
-    ).astype(BF16)
+    head_rows(sibling, corner)
 
 
 def finish_kernel(

time: 48.9 us -> 48.9 us (level)
  no operation moved by 1% of the time
where the time goes in v6:
time: 48.9 us; the launch traced here: 48.7 us
  Pallas kernels  48.1 us (98%)
  between operations  0.64 us (1%)
    pallas_call x1, Pallas kernels, fused_shards(): pl.pallas_call(step_kernel, out_shape=results, in_specs=[hbm] * 9 + [smem...  46.4 us
    pallas_call x1, Pallas kernels, fused_shards(): pl.pallas_call(finish_kernel, out_shape=results, in_specs=[hbm] * 3, out_...  1.74 us

profile of v6, /device:TPU:0, one launch (start us, length us, event | category | flops | bytes accessed | tf_op | source)
XLA Modules:
  0.0 48.7 jit_solution(15790384476743580399)
XLA Ops:
  0.6 46.4 %slide_step.1 = (bf16[192,192]{1,0:T(8,128)(2,1)}, bf16[48,1536]{1,0:T(8,128)(2,1)}, bf16[192,384]{1,0:T(8,128)(2,1)}) custom-call(bf16[192,384]{1,0:T(8,128)(2,1)} %features_hbm.1, bf16[192,384]{1,0:T(8,128)(2,1)} %outputs_hbm.1, bf16[384,1536]{1,0:T(8,128)(2,1)} %out_proj_hbm.1, f32[1536]{0:T(1024)} %layer_scale_hbm.1, f32[1536]{0:T(1024)} %tile_gain_hbm.1, ...), custom_call_target="tpu_custom_call" | custom-call | tf_op jit(solution)/shard_map/slide_step/pallas_call | solution.py:787
  47.0 1.7 %finish.1 = (bf16[192,192]{1,0:T(8,128)(2,1)}, bf16[48,1536]{1,0:T(8,128)(2,1)}, bf16[192,384]{1,0:T(8,128)(2,1)}) custom-call(bf16[192,192]{1,0:T(8,128)(2,1)} %get-tuple-element.6.heads_in, bf16[48,1536]{1,0:T(8,128)(2,1)} %get-tuple-element.7.tile_in, bf16[192,384]{1,0:T(8,128)(2,1)} %get-tuple-element.8.head_in), custom_call_target="tpu_custom_call" | custom-call | tf_op jit(solution)/shard_map/finish/pallas_call | solution.py:870
